TPU v7x, 32 devices: a whole 2x2x4 slice. The times are simulated.
32 devices in a mesh: leaf: 8 (over y, x, core), grid: 4 (over z).
Axes of the slice: x: 2, y: 2, z: 4, core: 2. Of those that a mesh axis runs over, the one named last changes fastest.
Arguments:
- child_front: float32 [8, 1, 2048, 4, 4, 128], P('leaf', None, None, None, 'grid'), as said below
- child_live: int32 [8, 1, 16], replicated, may hold values 0 or 1
- child_map: int32 [8, 1, 8], replicated, may hold values from 0 to 15, as said below
- parent_owner: int32 [4, 16], replicated, may hold values from 0 to 15, as said below
- parent_shift: float32 [8, 1, 2, 4, 128], P('leaf', None, None, 'grid'), may hold values from 0.5 to 2
Outputs:
- child_factor: float32 [8, 1, 2048, 2, 4, 128], P('leaf', None, None, None, 'grid')
- parent_done: float32 [8, 1, 2048, 2, 4, 128], P('leaf', None, None, None, 'grid')
Inputs may be any that keep to these rules, and one draw needn't show every extreme that they name: `child_map`: each row holds 8 different block numbers in increasing order, the last one being 15. `parent_owner`: each row is a permutation of the 16 slots. `child_front`: each front is symmetric positive definite.
All inputs are finite; a program needn't handle non-finite values.
Results may differ from a plain program's by a relative error of at most 0.0003.
Values sent between devices are 32-bit elements; how exact they have to be, the bound alone decides.
A program may use at most 128 MiB of HBM per device.

v0:
```python
import jax
import jax.numpy as jnp
from jax import lax
from jax.sharding import PartitionSpec as P

F = 2048
PIVOTS = 1024
NB = 128
CORDER = 1024
FB = 16
PB = 8
CB = 8


highest = lax.Precision.HIGHEST


def broadcast(value, axis, root):
    mine = lax.axis_index(axis) == root
    return lax.psum(jnp.where(mine, value, jnp.zeros_like(value)), axis)


def swapped_2(value, axis, distance):
    mask = 2**distance
    pairs = [(source, source ^ mask) for source in range(lax.axis_size(axis))]
    return lax.ppermute(value, axis, pairs)


def panel_factor(column_tail):
    lower_part = jnp.linalg.cholesky(column_tail[:, :NB])
    below_part = lax.linalg.triangular_solve(
        lower_part, column_tail[:, NB:], left_side=False, lower=True, transpose_a=True
    )
    return jnp.concatenate([lower_part, below_part], axis=1)


def apply_panel(front_cols, panel_cols, block_ids, panel):
    first_row = panel * NB
    pieces = []
    for round_pick in range(front_cols.shape[2]):
        target = block_ids[round_pick]
        offset = jnp.clip(target * NB - first_row, 0, F - first_row - NB)
        partner = lax.dynamic_slice_in_dim(panel_cols, offset, NB, 1)
        change = jnp.einsum("frn,fsn->frs", panel_cols, partner, precision=highest)
        current = front_cols[:, first_row:, round_pick, :]
        updated = jnp.where(target > panel, current - change, current)
        updated = jnp.where(target == panel, panel_cols, updated)
        upper_rows = jnp.where(target == panel, 0.0, front_cols[:, :first_row, round_pick, :])
        pieces.append(jnp.concatenate([upper_rows, updated], axis=1))
    return jnp.stack(pieces, axis=2)


def mask_front(front_cols, alive_mask, block_ids):
    live_rows = jnp.repeat(alive_mask, NB, axis=1)
    choose = (jnp.arange(FB)[:, None] == block_ids[None, :]).astype(jnp.float32)
    live_cols = jnp.dot(alive_mask, choose, precision=highest)
    places = block_ids[:, None] * NB + jnp.arange(NB)[None, :]
    diagonal = (jnp.arange(F)[:, None, None] == places[None]).astype(jnp.float32)
    kept = front_cols * live_rows[:, :, None, None] * live_cols[:, None, :, None]
    return kept + diagonal[None] * (1.0 - live_cols)[:, None, :, None]


def place_column(schur, targets, alive_mask, target):
    fronts = schur.shape[0]
    pick = (targets == target).astype(jnp.float32) * alive_mask
    tiles = schur.reshape(fronts, CORDER, CB, NB)
    column = jnp.einsum("fc,frcj->frj", pick, tiles, precision=highest)
    spread = (targets[:, None, :] == jnp.arange(FB)[None, :, None]).astype(
        jnp.float32
    ) * alive_mask[:, None, :]
    placed = jnp.einsum(
        "fbc,fcij->fbij", spread, column.reshape(fronts, CB, NB, NB), precision=highest
    )
    return placed.reshape(fronts, F, NB)


def body(child_front, child_live, child_map, parent_owner, parent_shift):
    grid_count = lax.axis_size("grid")
    grid_pos = lax.axis_index("grid")
    leaf_pos = lax.axis_index("leaf")
    member = leaf_pos % 2
    pair = leaf_pos // 2
    sibling = leaf_pos ^ 1
    fronts = child_front.shape[1]
    child_rounds = child_front.shape[3]
    pivot_rounds = PIVOTS // (NB * grid_count)
    parent_rounds = parent_shift.shape[2]
    my_alive = lax.dynamic_index_in_dim(child_live, leaf_pos, 0, keepdims=False).astype(jnp.float32)
    other_alive = lax.dynamic_index_in_dim(child_live, sibling, 0, keepdims=False).astype(
        jnp.float32
    )
    my_map = lax.dynamic_index_in_dim(child_map, leaf_pos, 0, keepdims=False)
    other_map = lax.dynamic_index_in_dim(child_map, sibling, 0, keepdims=False)
    child_blocks = jnp.arange(child_rounds) * grid_count + grid_pos
    front_cols = mask_front(
        child_front.reshape(fronts, F, child_rounds, NB), my_alive, child_blocks
    )
    for panel in range(PB):
        column = front_cols[:, :, panel // grid_count, :]
        outgoing = column
        arrived = broadcast(outgoing, "grid", panel % grid_count)
        column_tail = arrived[:, panel * NB :]
        front_cols = apply_panel(front_cols, panel_factor(column_tail), child_blocks, panel)
    child_factor = front_cols[:, :, :pivot_rounds, :]
    contrib = front_cols[:, PIVOTS:, pivot_rounds:, :]
    gathered = lax.all_gather(contrib[:, :, :, None, :], "grid", axis=3, tiled=True)
    mine_schur = gathered.reshape(fronts, CORDER, CORDER)
    other_schur = swapped_2(mine_schur, "leaf", 0)
    owner_row = lax.dynamic_index_in_dim(parent_owner, pair, 0, keepdims=False)
    slot_ids = (member * grid_count + grid_pos) * parent_rounds + jnp.arange(parent_rounds)
    holders = (owner_row[:, None] == slot_ids[None, :]).astype(jnp.int32)
    parent_blocks = jnp.sum(holders * jnp.arange(FB)[:, None], axis=0)
    shift_cols = parent_shift.reshape(fronts, parent_rounds, NB)
    my_live_contrib = my_alive[:, PB:]
    other_live_contrib = other_alive[:, PB:]
    pieces = []
    for round_pick in range(parent_rounds):
        target = parent_blocks[round_pick]
        column = place_column(mine_schur, my_map, my_live_contrib, target)
        column = column + place_column(other_schur, other_map, other_live_contrib, target)
        places = target * NB + jnp.arange(NB)
        diagonal = (jnp.arange(F)[:, None] == places[None, :]).astype(jnp.float32)
        pieces.append(column + diagonal[None] * shift_cols[:, round_pick, None, :])
    parent_cols = jnp.stack(pieces, axis=2)
    for panel in range(PB):
        holder = owner_row[panel]
        holder_side = holder // (grid_count * parent_rounds)
        holder_grid = holder // parent_rounds % grid_count
        holder_round = holder % parent_rounds
        column = lax.dynamic_index_in_dim(parent_cols, holder_round, 2, keepdims=False)
        outgoing = column
        arrived = broadcast(outgoing, "grid", holder_grid)
        swapped = swapped_2(arrived, "leaf", 0)
        received = jnp.where(member == holder_side, arrived, swapped)
        column_tail = received[:, panel * NB :]
        parent_cols = apply_panel(parent_cols, panel_factor(column_tail), parent_blocks, panel)
    upper_part = (jnp.arange(F) < PIVOTS)[None, :, None, None] & (parent_blocks >= PB)[
        None, None, :, None
    ]
    parent_cols = jnp.where(upper_part, 0.0, parent_cols)
    return (
        child_factor.reshape(1, fronts, F, pivot_rounds, 1, NB),
        parent_cols.reshape(1, fronts, F, parent_rounds, 1, NB),
    )


def solution(mesh):
    in_specs = (
        P("leaf", None, None, None, "grid", None),
        P(),
        P(),
        P(),
        P("leaf", None, None, "grid", None),
    )
    out_specs = (
        P("leaf", None, None, None, "grid", None),
        P("leaf", None, None, None, "grid", None),
    )
    return jax.shard_map(body, mesh=mesh, in_specs=in_specs, out_specs=out_specs, check_vma=False)
```

profile of v0, /device:TPU:0, one launch (start us, length us, event | category | flops | bytes accessed | tf_op | source)
XLA Modules:
  0.0 1644.8 jit_solution(5533225801638907985)
XLA Ops:
  8.9 10.9 copy.125
  19.8 3.0 fusion.1
  63.1 17.5 %all-reduce.17.cloned.1.call-done = f32[1,2048,128]{1,2,0:T(8,128)} async-done(((f32[1,2048,128]{1,2,0:T(8,128)}), f32[1,2048,128]{1,2,0:T(8,128)}) %all-reduce.17.cloned.1.call-update) | async-done | bytes 1048592 | tf_op jit(solution)/shard_map/psum | solution.py:20
  82.4 11.7 custom-call.50
  95.7 9.8 custom-call.51
  111.5 2.6 fusion.136
  116.7 46.0 %all-reduce.19.cloned.1.call-done = f32[1,2048,128]{1,2,0:T(8,128)} async-done(((f32[1,2048,128]{1,2,0:T(8,128)}), f32[1,2048,128]{1,2,0:T(8,128)}) %all-reduce.19.cloned.1.call-update) | async-done | bytes 1048592 | tf_op jit(solution)/shard_map/psum | solution.py:20
  164.4 11.7 custom-call.52
  177.8 9.8 custom-call.53
  199.4 44.0 %all-reduce.21.cloned.1.call-done = f32[1,2048,128]{1,2,0:T(8,128)} async-done(((f32[1,2048,128]{1,2,0:T(8,128)}), f32[1,2048,128]{1,2,0:T(8,128)}) %all-reduce.21.cloned.1.call-update) | async-done | bytes 1048592 | tf_op jit(solution)/shard_map/psum | solution.py:20
  245.3 11.7 custom-call.54
  258.6 9.8 custom-call.55
  279.3 45.3 %all-reduce.23.cloned.1.call-done = f32[1,2048,128]{1,2,0:T(8,128)} async-done(((f32[1,2048,128]{1,2,0:T(8,128)}), f32[1,2048,128]{1,2,0:T(8,128)}) %all-reduce.23.cloned.1.call-update) | async-done | bytes 1048592 | tf_op jit(solution)/shard_map/psum | solution.py:20
  326.3 11.7 custom-call.56
  339.6 9.8 custom-call.57
  360.2 46.3 %all-reduce.25.cloned.1.call-done = f32[1,2048,128]{1,2,0:T(8,128)} async-done(((f32[1,2048,128]{1,2,0:T(8,128)}), f32[1,2048,128]{1,2,0:T(8,128)}) %all-reduce.25.cloned.1.call-update) | async-done | bytes 1048592 | tf_op jit(solution)/shard_map/psum | solution.py:20
  408.3 11.7 custom-call.58
  421.7 9.8 custom-call.59
  445.0 43.6 %all-reduce.27.cloned.1.call-done = f32[1,2048,128]{1,2,0:T(8,128)} async-done(((f32[1,2048,128]{1,2,0:T(8,128)}), f32[1,2048,128]{1,2,0:T(8,128)}) %all-reduce.27.cloned.1.call-update) | async-done | bytes 1048592 | tf_op jit(solution)/shard_map/psum | solution.py:20
  490.3 11.7 custom-call.60
  503.7 9.8 custom-call.61
  526.5 43.8 %all-reduce.29.cloned.1.call-done = f32[1,2048,128]{1,2,0:T(8,128)} async-done(((f32[1,2048,128]{1,2,0:T(8,128)}), f32[1,2048,128]{1,2,0:T(8,128)}) %all-reduce.29.cloned.1.call-update) | async-done | bytes 1048592 | tf_op jit(solution)/shard_map/psum | solution.py:20
  572.1 11.7 custom-call.62
  585.5 9.8 custom-call.63
  608.6 43.3 %all-reduce.31.cloned.1.call-done = f32[1,2048,128]{1,2,0:T(8,128)} async-done(((f32[1,2048,128]{1,2,0:T(8,128)}), f32[1,2048,128]{1,2,0:T(8,128)}) %all-reduce.31.cloned.1.call-update) | async-done | bytes 1048592 | tf_op jit(solution)/shard_map/psum | solution.py:20
  653.7 11.7 custom-call.64
  667.1 10.4 custom-call.65
  683.8 79.8 %all-gather.3.cloned.1.call-done = f32[1,1024,2,512]{1,3,2,0:T(8,128)} async-done(((f32[1,1024,2,128]{1,3,2,0:T(8,128)}), f32[1,1024,2,512]{1,3,2,0:T(8,128)}) %all-gather.3.cloned.1.call-update) | async-done | bytes 4194320 | tf_op jit(solution)/shard_map/all_gather | solution.py:106
  772.5 5.4 copy.301
  777.9 7.2 fusion.560
  787.3 5.2 fusion.566
  794.8 5.6 copy.302
  800.4 7.2 fusion.569
  807.6 6.0 fusion.563
  815.8 2.8 copy.191
  818.6 3.6 convolution_add_fusion.1
  822.2 2.8 copy.190
  834.0 50.4 %all-reduce.33.cloned.1.call-done = f32[1,2048,128]{1,2,0:T(8,128)} async-done(((f32[1,2048,128]{1,2,0:T(8,128)}), f32[1,2048,128]{1,2,0:T(8,128)}) %all-reduce.33.cloned.1.call-update) | async-done | bytes 1048592 | tf_op jit(solution)/shard_map/psum | solution.py:20
  895.6 13.2 custom-call.66
  915.6 11.3 custom-call.67
  929.2 2.8 fusion.130
  936.3 51.0 %all-reduce.35.cloned.1.call-done = f32[1,2048,128]{1,2,0:T(8,128)} async-done(((f32[1,2048,128]{1,2,0:T(8,128)}), f32[1,2048,128]{1,2,0:T(8,128)}) %all-reduce.35.cloned.1.call-update) | async-done | bytes 1048592 | tf_op jit(solution)/shard_map/psum | solution.py:20
  1001.2 13.2 custom-call.68
  1021.1 11.3 custom-call.69
  1041.7 51.3 %all-reduce.37.cloned.1.call-done = f32[1,2048,128]{1,2,0:T(8,128)} async-done(((f32[1,2048,128]{1,2,0:T(8,128)}), f32[1,2048,128]{1,2,0:T(8,128)}) %all-reduce.37.cloned.1.call-update) | async-done | bytes 1048592 | tf_op jit(solution)/shard_map/psum | solution.py:20
  1106.9 13.2 custom-call.70
  1126.8 11.3 custom-call.71
  1147.1 51.2 %all-reduce.39.cloned.1.call-done = f32[1,2048,128]{1,2,0:T(8,128)} async-done(((f32[1,2048,128]{1,2,0:T(8,128)}), f32[1,2048,128]{1,2,0:T(8,128)}) %all-reduce.39.cloned.1.call-update) | async-done | bytes 1048592 | tf_op jit(solution)/shard_map/psum | solution.py:20
  1212.7 13.2 custom-call.72
  1232.6 11.3 custom-call.73
  1252.9 51.0 %all-reduce.41.cloned.1.call-done = f32[1,2048,128]{1,2,0:T(8,128)} async-done(((f32[1,2048,128]{1,2,0:T(8,128)}), f32[1,2048,128]{1,2,0:T(8,128)}) %all-reduce.41.cloned.1.call-update) | async-done | bytes 1048592 | tf_op jit(solution)/shard_map/psum | solution.py:20
  1318.2 13.2 custom-call.74
  1338.1 11.3 custom-call.75
  1378.2 31.1 %all-reduce.43.cloned.1.call-done = f32[1,2048,128]{1,2,0:T(8,128)} async-done(((f32[1,2048,128]{1,2,0:T(8,128)}), f32[1,2048,128]{1,2,0:T(8,128)}) %all-reduce.43.cloned.1.call-update) | async-done | bytes 1048592 | tf_op jit(solution)/shard_map/psum | solution.py:20
  1419.2 11.7 custom-call.76
  1432.5 9.8 custom-call.77
  1456.4 45.4 %all-reduce.45.cloned.1.call-done = f32[1,2048,128]{1,2,0:T(8,128)} async-done(((f32[1,2048,128]{1,2,0:T(8,128)}), f32[1,2048,128]{1,2,0:T(8,128)}) %all-reduce.45.cloned.1.call-update) | async-done | bytes 1048592 | tf_op jit(solution)/shard_map/psum | solution.py:20
  1509.3 11.7 custom-call.78
  1522.8 9.8 custom-call.79
  1545.9 44.9 %all-reduce.47.cloned.1.call-done = f32[1,2048,128]{1,2,0:T(8,128)} async-done(((f32[1,2048,128]{1,2,0:T(8,128)}), f32[1,2048,128]{1,2,0:T(8,128)}) %all-reduce.47.cloned.1.call-update) | async-done | bytes 1048592 | tf_op jit(solution)/shard_map/psum | solution.py:20
  1594.4 6.0 copy.241
  1605.3 11.7 custom-call.80
  1618.4 9.8 custom-call.81
  1634.2 3.6 copy.242
  (576 shorter events, 322.4 us)
Async XLA Ops:
  7.2 756.5 %copy-start = (s32[4,16]{1,0:T(4,128)S(1)}, s32[4,16]{1,0:T(4,128)}, u32[]{:S(2)}) copy-start(s32[4,16]{1,0:T(4,128)} %param.25) | copy-start | bytes 772
  7.2 73.4 %all-reduce.17.cloned.1.call-start = ((), (), s32[]{:S(2)}) async-start(), calls=%async_computation | async-start | bytes 2097152 | tf_op jit(solution)/shard_map/psum | solution.py:20
  25.9 136.8 %all-reduce.19.cloned.1.call-start = ((), (), s32[]{:S(2)}) async-start(), calls=%async_computation.1 | async-start | bytes 2097152 | tf_op jit(solution)/shard_map/psum | solution.py:20
  111.2 132.2 %all-reduce.21.cloned.1.call-start = ((), (), s32[]{:S(2)}) async-start(), calls=%async_computation.2 | async-start | bytes 2097152 | tf_op jit(solution)/shard_map/psum | solution.py:20
  192.1 132.4 %all-reduce.23.cloned.1.call-start = ((), (), s32[]{:S(2)}) async-start(), calls=%async_computation.3 | async-start | bytes 2097152 | tf_op jit(solution)/shard_map/psum | solution.py:20
  198.7 71.8 %copy-start.52 = (f32[1,2048,1,128]{1,3,2,0:T(8,128)}, f32[1,2048,1,128]{1,3,2,0:T(8,128)S(1)}, u32[]{:S(2)}) copy-start(f32[1,2048,1,128]{1,3,2,0:T(8,128)S(1)} %maximum_bitcast_fusion.2) | copy-start | bytes 3145732
  273.2 133.4 %all-reduce.25.cloned.1.call-start = ((), (), s32[]{:S(2)}) async-start(), calls=%async_computation.4 | async-start | bytes 2097152 | tf_op jit(solution)/shard_map/psum | solution.py:20
  355.2 133.4 %all-reduce.27.cloned.1.call-start = ((), (), s32[]{:S(2)}) async-start(), calls=%async_computation.5 | async-start | bytes 2097152 | tf_op jit(solution)/shard_map/psum | solution.py:20
  356.6 51.8 %copy-start.35 = (f32[1,2048,1,128]{1,3,2,0:T(8,128)}, f32[1,2048,1,128]{1,3,2,0:T(8,128)S(1)}, u32[]{:S(2)}) copy-start(f32[1,2048,1,128]{1,3,2,0:T(8,128)S(1)} %maximum_bitcast_fusion.11) | copy-start | bytes 3145732
  358.4 73.1 %copy-start.37 = (f32[1,2048,1,128]{1,3,2,0:T(8,128)}, f32[1,2048,1,128]{1,3,2,0:T(8,128)S(1)}, u32[]{:S(2)}) copy-start(f32[1,2048,1,128]{1,3,2,0:T(8,128)S(1)} %maximum_bitcast_fusion.18) | copy-start | bytes 3145732
  433.4 4.2 copy-start.36
  437.2 133.2 %all-reduce.29.cloned.1.call-start = ((), (), s32[]{:S(2)}) async-start(), calls=%async_computation.6 | async-start | bytes 2097152 | tf_op jit(solution)/shard_map/psum | solution.py:20
  519.0 133.0 %all-reduce.31.cloned.1.call-start = ((), (), s32[]{:S(2)}) async-start(), calls=%async_computation.7 | async-start | bytes 2097152 | tf_op jit(solution)/shard_map/psum | solution.py:20
  521.2 51.0 %copy-start.33 = (f32[1,2048,1,128]{1,3,2,0:T(8,128)}, f32[1,2048,1,128]{1,3,2,0:T(8,128)S(1)}, u32[]{:S(2)}) copy-start(f32[1,2048,1,128]{1,3,2,0:T(8,128)S(1)} %maximum_bitcast_fusion.13) | copy-start | bytes 3145732
  583.9 15.1 copy-start.73
  585.4 17.4 %copy-start.6 = (f32[1,128,128]{1,2,0:T(8,128)}, f32[1,128,128]{1,2,0:T(8,128)S(1)}, u32[]{:S(2)}) copy-start(f32[1,128,128]{1,2,0:T(8,128)S(1)} %get-tuple-element.34) | copy-start | bytes 196612
  600.6 163.1 %all-gather.3.cloned.1.call-start = ((), (), s32[]{:S(2)}) async-start(), calls=%async_computation.16 | async-start | bytes 5242880 | tf_op jit(solution)/shard_map/all_gather | solution.py:106
  600.8 5.8 copy-start.71
  677.5 4.5 copy-start.68
  682.0 89.3 %copy-start.100 = (f32[1,1,2,1,128]{4,3,2,1,0:T(1,128)S(1)}, f32[1,1,2,1,128]{4,3,2,1,0:T(1,128)}, u32[]{:S(2)}) copy-start(f32[1,1,2,1,128]{4,3,2,1,0:T(1,128)} %param.26) | copy-start | bytes 3076
  683.4 201.0 %all-reduce.33.cloned.1.call-start = ((), (), s32[]{:S(2)}) async-start(), calls=%async_computation.8 | async-start | bytes 2097152 | tf_op jit(solution)/shard_map/psum | solution.py:20
  763.7 31.1 %collective-permute-start = (f32[1,1024,1024]{1,2,0:T(8,128)}, f32[1,1024,1024]{1,2,0:T(8,128)}, u32[]{:S(2)}, u32[]{:S(2)}) collective-permute-start(f32[1,1024,1024]{1,2,0:T(8,128)} %bitcast.1359), channel_id=1, source_target_pairs={{0,4},{4,0},{8,12},{12,8},{16,20},{20,16},{24,28},{28,24},{1,5},{5... | collective-permute-start | bytes 12582920 | tf_op jit(solution)/shard_map/ppermute | solution.py:26
  777.9 7.2 copy-start.92
  777.9 7.2 copy-start.93
  777.9 9.4 copy-start.2
  800.4 7.2 copy-start.3
  800.4 13.2 copy-start.32
  818.6 11.1 copy-start.94
  818.6 11.1 copy-start.98
  822.2 9.0 copy-start.95
  822.2 9.0 copy-start.99
  833.7 153.6 %all-reduce.35.cloned.1.call-start = ((), (), s32[]{:S(2)}) async-start(), calls=%async_computation.9 | async-start | bytes 2097152 | tf_op jit(solution)/shard_map/psum | solution.py:20
  884.4 5.2 collective-permute-start.1
  926.9 5.2 copy-start.14
  926.9 5.2 copy-start.59
  935.8 157.1 %all-reduce.37.cloned.1.call-start = ((), (), s32[]{:S(2)}) async-start(), calls=%async_computation.10 | async-start | bytes 2097152 | tf_op jit(solution)/shard_map/psum | solution.py:20
  987.3 7.8 collective-permute-start.2
  1032.4 4.7 copy-start.13
  1032.4 4.7 copy-start.60
  1041.4 156.9 %all-reduce.39.cloned.1.call-start = ((), (), s32[]{:S(2)}) async-start(), calls=%async_computation.11 | async-start | bytes 2097152 | tf_op jit(solution)/shard_map/psum | solution.py:20
  1092.9 8.0 collective-permute-start.3
  1138.0 4.5 copy-start.28
  1138.0 4.5 copy-start.61
  1146.9 157.1 %all-reduce.41.cloned.1.call-start = ((), (), s32[]{:S(2)}) async-start(), calls=%async_computation.12 | async-start | bytes 2097152 | tf_op jit(solution)/shard_map/psum | solution.py:20
  1198.3 8.3 collective-permute-start.4
  1243.8 4.4 copy-start.9
  1243.8 4.4 copy-start.62
  1252.5 156.9 %all-reduce.43.cloned.1.call-start = ((), (), s32[]{:S(2)}) async-start(), calls=%async_computation.13 | async-start | bytes 2097152 | tf_op jit(solution)/shard_map/psum | solution.py:20
  1304.0 8.3 collective-permute-start.5
  1349.4 4.2 copy-start.63
  1354.6 23.5 %copy-start.97 = (s32[2]{0:T(128)S(1)}, s32[2]{0:T(128)}, u32[]{:S(2)}) copy-start(s32[2]{0:T(128)} %copy-done.96) | copy-start | bytes 28
  1357.9 144.0 %all-reduce.45.cloned.1.call-start = ((), (), s32[]{:S(2)}) async-start(), calls=%async_computation.14 | async-start | bytes 2097152 | tf_op jit(solution)/shard_map/psum | solution.py:20
  1409.3 7.8 copy-start.78
  1409.3 7.8 collective-permute-start.6
  1442.3 4.9 copy-start.76
  1450.5 140.3 %all-reduce.47.cloned.1.call-start = ((), (), s32[]{:S(2)}) async-start(), calls=%async_computation.15 | async-start | bytes 2097152 | tf_op jit(solution)/shard_map/psum | solution.py:20
  1453.8 50.2 %copy-start.7 = (f32[1,128,128]{1,2,0:T(8,128)S(1)}, f32[1,128,128]{1,2,0:T(8,128)}, u32[]{:S(2)}) copy-start(f32[1,128,128]{1,2,0:T(8,128)} %copy-done.6) | copy-start | bytes 196612
  1456.4 49.3 %copy-start.18 = (f32[1,2048,1,128]{1,3,2,0:T(8,128)S(1)}, f32[1,2048,1,128]{1,3,2,0:T(8,128)}, u32[]{:S(2)}) copy-start(f32[1,2048,1,128]{1,3,2,0:T(8,128)} %copy-done.17) | copy-start | bytes 3145732
  1456.4 50.1 %copy-start.16 = (f32[1,2048,1,128]{1,3,2,0:T(8,128)S(1)}, f32[1,2048,1,128]{1,3,2,0:T(8,128)}, u32[]{:S(2)}) copy-start(f32[1,2048,1,128]{1,3,2,0:T(8,128)} %copy-done.15) | copy-start | bytes 3145732
  1501.9 5.4 copy-start.79
  1501.9 5.4 collective-permute-start.7
  1590.8 11.2 collective-permute-start.8
  1592.9 7.5 copy-start.23
  1632.8 5.0 copy-start.1
  (63 other events, 125.2 us)
Sparse Core Ops, SparseCore 0:
  26.0 54.5 all-reduce.16
  111.4 51.2 all-reduce.18
  192.2 51.1 all-reduce.20
  273.3 51.1 all-reduce.22
  355.3 51.1 all-reduce.24
  437.3 51.1 all-reduce.26
  519.1 51.2 all-reduce.28
  600.7 51.1 all-reduce.30
  683.5 80.1 all-gather.2
  833.9 50.4 all-reduce.32
  936.0 51.3 all-reduce.34
  1041.6 51.3 all-reduce.36
  1147.0 51.3 all-reduce.38
  1252.6 51.3 all-reduce.40
  1358.0 51.3 all-reduce.42
  1450.6 51.2 all-reduce.44
  1539.6 51.2 all-reduce.46
where the time goes:
time: 1660 us; the launch traced here: 1640 us
  waiting for transfers between devices  786 us (47%)
  other arithmetic  500 us (30%)
  matrix products  141 us (8%)
  local copies, waits for them, and re-layouts  111 us (7%)
  between operations  102 us (6%)
    psum x16, waiting for transfers between devices, broadcast(): return lax.psum(jnp.where(mine, value, jnp.zeros_like(value)), axis)  706 us
    another operation x48, other arithmetic, panel_factor(): lower_part = jnp.linalg.cholesky(column_tail[:, :NB])  211 us
    another operation x32, other arithmetic, panel_factor(): lax.linalg.triangular_solve(lower_part, column_tail[:, NB:], left_side=Fa...  182 us
    all_gather x1, waiting for transfers between devices, body(): lax.all_gather(contrib[:, :, :, None, :], 'grid', axis=3, tiled=True)  79.8 us
    dot_general x48, matrix products, apply_panel(): change = jnp.einsum('frn,fsn->frs', panel_cols, partner, precision=highest)  72.9 us
    unnamed x205, local copies, waits for them, and re-layouts  48.8 us
  transfers between devices with their start and end apart: 26, of which 17 were waited for; matrix products, arithmetic and copies ran while one was open for 7% of the time, Pallas kernels for 0%

commit v1 on v0

v1 whole, which is shorter than its diff:
```python
import functools

import jax
import jax.numpy as jnp
from jax import lax
from jax.experimental import pallas as pl
from jax.experimental.pallas import tpu as pltpu
from jax.sharding import PartitionSpec as P

F = 2048
PIVOTS = 1024
NB = 128
FB = 16
PB = 8
CB = 8
CHUNK = 512
PAIR = 256
f32 = jnp.float32
bf16 = jnp.bfloat16
NT = (((1,), (1,)), ((), ()))
VMEM = pl.BlockSpec(memory_space=pltpu.VMEM)
SMEM = pl.BlockSpec(memory_space=pltpu.SMEM)
LIMIT = 56 * 1024 * 1024


def split(value):
    high = value.astype(bf16)
    return high, (value - high.astype(f32)).astype(bf16)


def times(a_high, a_low, b_high, b_low):
    def dot(a, b):
        return lax.dot_general(a, b, NT, preferred_element_type=f32)

    return dot(a_high, b_high) + (dot(a_low, b_high) + dot(a_high, b_low))


def rows_of(index, count):
    return pl.ds(pl.multiple_of(index * count, count), count)


def block_inverse(block_ref, inverse_ref):
    lane = lax.broadcasted_iota(jnp.int32, (8, NB), 1)
    sub = lax.broadcasted_iota(jnp.int32, (8, NB), 0)
    groups = NB // 8
    left = [block_ref[8 * g : 8 * g + 8, :] for g in range(groups)]
    right = [jnp.where(lane == sub + 8 * g, 1.0, 0.0).astype(f32) for g in range(groups)]
    for step in range(NB):
        g, j = divmod(step, 8)
        column = jnp.broadcast_to(left[g][:, step : step + 1], (8, NB))
        pivot = jnp.broadcast_to(column[j : j + 1, :], (8, NB))
        scale = 1.0 / pivot
        row_left = jnp.broadcast_to(left[g][j : j + 1, :], (8, NB)) * scale
        row_right = jnp.broadcast_to(right[g][j : j + 1, :], (8, NB)) * scale
        diagonal = pivot if j == 0 else jnp.where(sub >= j, pivot, diagonal)
        if j < 7:
            below = jnp.where(sub > j, column, 0.0)
            left[g] = left[g] - below * row_left
            right[g] = right[g] - below * row_right
        for v in range(g + 1, groups):
            column = jnp.broadcast_to(left[v][:, step : step + 1], (8, NB))
            left[v] = left[v] - column * row_left
            right[v] = right[v] - column * row_right
        if j == 7:
            inverse_ref[8 * g : 8 * g + 8, :] = right[g] * lax.rsqrt(diagonal)


def factor_blocks(front, high, low, block, inverse, count, height, emit):
    chunks = height // CHUNK
    block[...] = front[0, 0:NB, 0:NB]

    def solve(panel, pair, first):
        cols = slice(first, first + NB)
        inv_high, inv_low = split(inverse[...])

        def one(k, carry):
            rows = rows_of(k, CHUNK)
            value = times(*split(front[pair, rows, cols]), inv_high, inv_low)
            place = lax.broadcasted_iota(jnp.int32, (CHUNK, NB), 0) + (k * CHUNK - panel * NB)
            value = jnp.where(place >= lax.broadcasted_iota(jnp.int32, (CHUNK, NB), 1), value, 0.0)
            value_high, value_low = split(value)
            high[pair, rows, cols] = value_high
            low[pair, rows, cols] = value_low
            emit(panel, rows, value)
            return carry

        lax.fori_loop(panel * NB // CHUNK, chunks, one, 0)

    def step(panel, carry):
        pair = panel // 2
        block_inverse(block, inverse)

        @pl.when(panel % 2 == 0)
        def _():
            solve(panel, pair, 0)
            next_rows = rows_of(panel + 1, NB)
            part_high = high[pair, next_rows, 0:NB]
            part_low = low[pair, next_rows, 0:NB]

            def one(k, carry):
                rows = rows_of(k, CHUNK)
                front[pair, rows, NB:PAIR] -= times(
                    high[pair, rows, 0:NB], low[pair, rows, 0:NB], part_high, part_low
                )
                return carry

            lax.fori_loop(panel * NB // CHUNK, chunks, one, 0)
            block[...] = front[pair, next_rows, NB:PAIR]

        @pl.when(panel % 2 == 1)
        def _():
            solve(panel, pair, NB)

            def column(q, carry):
                part_high = high[pair, rows_of(q, PAIR), :]
                part_low = low[pair, rows_of(q, PAIR), :]

                def one(k, carry):
                    rows = rows_of(k, CHUNK)
                    front[q, rows, :] -= times(high[pair, rows, :], low[pair, rows, :], part_high, part_low)
                    return carry

                lax.fori_loop(q * PAIR // CHUNK, chunks, one, 0)
                return carry

            lax.fori_loop(pair + 1, count // 2, column, 0)

            @pl.when(pair + 1 < count // 2)
            def _():
                block[...] = front[pair + 1, rows_of(panel + 1, NB), 0:NB]

        return carry

    lax.fori_loop(0, count, step, 0)


def masked(value, live_row, live_col, same):
    row = lax.broadcasted_iota(jnp.int32, (NB, NB), 0)
    col = lax.broadcasted_iota(jnp.int32, (NB, NB), 1)
    kept = jnp.where(live_row * live_col > 0, value, 0.0)
    alone = jnp.where(same & (live_row == 0), 1.0, 0.0)
    return kept + jnp.where(row == col, alone, 0.0)


def child_kernel(index, grid_count, live, place, entries, *rest):
    done = rest[: 2 * index]
    own, high, low, front, block, inverse = rest[2 * index :]
    base = index * grid_count * NB
    height = F - base
    own[...] = jnp.zeros_like(own)

    def load(q, carry):
        for half in range(2):
            col = 2 * q + half
            live_col = live[index * grid_count + col]
            for r in range(height // NB):
                front[q, r * NB : (r + 1) * NB, half * NB : (half + 1) * NB] = masked(
                    entries[col, r * NB : (r + 1) * NB, :], live[base // NB + r], live_col, col == r
                )
        return carry

    lax.fori_loop(0, grid_count // 2, load, 0)
    for earlier in range(index):
        past_high, past_low = done[2 * earlier], done[2 * earlier + 1]
        offset = (index - earlier) * grid_count * NB

        def column(q, carry):
            def pairs(p, carry):
                near = pl.ds(pl.multiple_of(offset + q * PAIR, PAIR), PAIR)
                part_high, part_low = past_high[p, near, :], past_low[p, near, :]

                def one(k, carry):
                    rows = pl.ds(pl.multiple_of(offset + k * CHUNK, CHUNK), CHUNK)
                    front[q, rows_of(k, CHUNK), :] -= times(
                        past_high[p, rows, :], past_low[p, rows, :], part_high, part_low
                    )
                    return carry

                return lax.fori_loop(q * PAIR // CHUNK, height // CHUNK, one, carry)

            return lax.fori_loop(0, grid_count // 2, pairs, carry)

        lax.fori_loop(0, grid_count // 2, column, 0)

    def emit(panel, rows, value):
        @pl.when(panel == place[0])
        def _():
            own[pl.ds(pl.multiple_of(rows.start + base, NB), rows.size), :] = value

    factor_blocks(front, high, low, block, inverse, grid_count, height, emit)


def schur_kernel(rounds, pivot_rounds, grid_count, live, *rest):
    late = rounds - pivot_rounds
    entries = rest[:late]
    done = rest[late : late + 2 * pivot_rounds]
    (out,) = rest[late + 2 * pivot_rounds :]
    for q in range(CB // 2):
        source = 2 * q // grid_count
        inner = 2 * q % grid_count
        shift = source * grid_count * NB

        def tile(k, carry):
            total = None
            for index in range(pivot_rounds):
                past_high, past_low = done[2 * index], done[2 * index + 1]
                offset = PIVOTS - index * grid_count * NB
                rows = pl.ds(pl.multiple_of(offset + k * PAIR, PAIR), PAIR)
                near = slice(offset + q * PAIR, offset + (q + 1) * PAIR)
                for p in range(grid_count // 2):
                    product = times(
                        past_high[p, rows, :], past_low[p, rows, :], past_high[p, near, :], past_low[p, near, :]
                    )
                    total = product if total is None else total + product
            for row in range(2):
                for col in range(2):
                    r = 2 * k + row
                    c = 2 * q + col
                    value = entries[source][inner + col, pl.ds(pl.multiple_of(r * NB - shift, NB), NB), :]
                    value = masked(value, live[PB + r], live[PB + c], r == c)
                    part = total[row * NB : (row + 1) * NB, col * NB : (col + 1) * NB]
                    out[c, rows_of(r, NB), :] = value - part
            return carry

        lax.fori_loop(q, CB // 2, tile, 0)


def parent_kernel(slots, blocks, mine_at, other_at, mine, other, diagonal, own, front, high, low, block, inverse):
    row_id = lax.broadcasted_iota(jnp.int32, (NB, NB), 0)
    col_id = lax.broadcasted_iota(jnp.int32, (NB, NB), 1)
    own[...] = jnp.zeros_like(own)

    def extension(schur, at, r, b, turn):
        cr, cb = at[r], at[b]
        present = (cr >= 0) & (cb >= 0)
        cr, cb = jnp.maximum(cr, 0), jnp.maximum(cb, 0)
        if not turn:
            value = schur[cb, rows_of(cr, NB), :]
        else:
            value = schur[jnp.minimum(cr, cb), rows_of(jnp.maximum(cr, cb), NB), :]
            value = jnp.where(cr >= cb, value, value.T)
        return jnp.where(present, value, 0.0)

    def assembled(r, b, turn):
        start = jnp.where((row_id == col_id) & (r == b), diagonal[pl.ds(b, 1), :], 0.0)
        return start + extension(mine, mine_at, r, b, turn) + extension(other, other_at, r, b, turn)

    def load(q, carry):
        for half in range(2):
            b = 2 * q + half

            def one(r, carry):
                front[q, rows_of(r, NB), half * NB : (half + 1) * NB] = assembled(r, b, False)
                return carry

            lax.fori_loop(b, FB, one, 0)
        return carry

    lax.fori_loop(0, PB // 2, load, 0)

    def emit(panel, rows, value):
        for s in range(slots):

            @pl.when(blocks[s] == panel)
            def _():
                own[s, rows, :] = value

    factor_blocks(front, high, low, block, inverse, PB, F, emit)

    def finish(s, carry):
        b = blocks[s]

        @pl.when(b >= PB)
        def _():
            def one(r, carry):
                own[s, rows_of(r, NB), :] = assembled(r, b, True)
                return carry

            lax.fori_loop(PB, FB, one, 0)
            near = rows_of(b, NB)

            def part(k, carry):
                rows = rows_of(k, CHUNK)
                total = None
                for p in range(PB // 2):
                    product = times(high[p, rows, :], low[p, rows, :], high[p, near, :], low[p, near, :])
                    total = product if total is None else total + product
                own[s, rows, :] -= total
                return carry

            lax.fori_loop(PIVOTS // CHUNK, F // CHUNK, part, 0)

        return carry

    lax.fori_loop(0, slots, finish, 0)


def call(kernel, outs, scratch, smem, vmem, flops):
    size = sum(a.size * a.dtype.itemsize for a in vmem) + sum(a.size * a.dtype.itemsize for a in outs)
    return pl.pallas_call(
        kernel,
        out_shape=outs,
        in_specs=[SMEM] * len(smem) + [VMEM] * len(vmem),
        out_specs=[VMEM] * len(outs),
        scratch_shapes=scratch,
        compiler_params=pltpu.CompilerParams(vmem_limit_bytes=LIMIT),
        cost_estimate=pl.CostEstimate(flops=flops, bytes_accessed=size, transcendentals=0),
    )(*smem, *vmem)


def shape(dims, dtype=f32):
    return jax.ShapeDtypeStruct(dims, dtype)


def body(child_front, child_live, child_map, parent_owner, parent_shift):
    grid_count = lax.axis_size("grid")
    leaf_count = lax.axis_size("leaf")
    grid_pos = lax.axis_index("grid")
    leaf_pos = lax.axis_index("leaf")
    member = leaf_pos % 2
    sibling = leaf_pos ^ 1
    rounds = child_front.shape[3]
    pivot_rounds = PIVOTS // (NB * grid_count)
    slots = parent_shift.shape[2]
    swap = [(source, source ^ 1) for source in range(leaf_count)]
    entries = child_front.reshape(F, rounds, NB)
    shifts = lax.all_gather(parent_shift.reshape(slots, NB), "grid", axis=0)
    gathered = [
        lax.all_gather(entries[t * grid_count * NB :, t, :], "grid", axis=0) for t in range(rounds)
    ]

    my_live = lax.dynamic_index_in_dim(child_live, leaf_pos, 0, keepdims=False)[0]
    other_live = lax.dynamic_index_in_dim(child_live, sibling, 0, keepdims=False)[0]
    my_map = lax.dynamic_index_in_dim(child_map, leaf_pos, 0, keepdims=False)[0]
    other_map = lax.dynamic_index_in_dim(child_map, sibling, 0, keepdims=False)[0]

    def sources(targets, alive):
        hit = (targets[None, :] == jnp.arange(FB)[:, None]) & (alive[None, PB:] > 0)
        return jnp.sum(jnp.where(hit, jnp.arange(1, CB + 1)[None, :], 0), axis=1).astype(jnp.int32) - 1

    owner_row = lax.dynamic_index_in_dim(parent_owner, leaf_pos // 2, 0, keepdims=False)
    slot_ids = (member * grid_count + grid_pos) * slots + jnp.arange(slots)
    holders = (owner_row[:, None] == slot_ids[None, :]).astype(jnp.int32)
    parent_blocks = jnp.sum(holders * jnp.arange(FB)[:, None], axis=0).astype(jnp.int32)
    other_shifts = lax.ppermute(shifts, "leaf", swap)
    first = jnp.where(member == 0, shifts, other_shifts)
    second = jnp.where(member == 0, other_shifts, shifts)
    by_slot = jnp.concatenate([first, second], axis=0).reshape(FB, NB)
    chosen = owner_row[:, None, None] == jnp.arange(FB)[None, :, None]
    diagonal = jnp.sum(jnp.where(chosen, by_slot[None], 0.0), axis=1)

    place = grid_pos.astype(jnp.int32).reshape(1)
    owned = []
    done = []
    for t in range(pivot_rounds):
        height = F - t * grid_count * NB
        packed = (grid_count // 2, height, PAIR)
        own, high, low = call(
            functools.partial(child_kernel, t, grid_count),
            [shape((F, NB)), shape(packed, bf16), shape(packed, bf16)],
            [pltpu.VMEM(packed, f32), pltpu.VMEM((NB, NB), f32), pltpu.VMEM((NB, NB), f32)],
            [my_live, place],
            [gathered[t], *done],
            25_000_000_000,
        )
        owned.append(own)
        done += [high, low]
    (mine,) = call(
        functools.partial(schur_kernel, rounds, pivot_rounds, grid_count),
        [shape((CB, F - PIVOTS, NB))],
        [],
        [my_live],
        [*gathered[pivot_rounds:], *done],
        6_000_000_000,
    )
    other = lax.ppermute(mine, "leaf", swap)
    packed = (PB // 2, F, PAIR)
    (parent,) = call(
        functools.partial(parent_kernel, slots),
        [shape((slots, F, NB))],
        [
            pltpu.VMEM(packed, f32),
            pltpu.VMEM(packed, bf16),
            pltpu.VMEM(packed, bf16),
            pltpu.VMEM((NB, NB), f32),
            pltpu.VMEM((NB, NB), f32),
        ],
        [parent_blocks, sources(my_map, my_live), sources(other_map, other_live)],
        [mine, other, diagonal],
        50_000_000_000,
    )
    child_factor = jnp.stack(owned, axis=1)
    parent_done = jnp.swapaxes(parent, 0, 1)
    return (
        child_factor.reshape(1, 1, F, pivot_rounds, 1, NB),
        parent_done.reshape(1, 1, F, slots, 1, NB),
    )


def solution(mesh):
    in_specs = (
        P("leaf", None, None, None, "grid", None),
        P(),
        P(),
        P(),
        P("leaf", None, None, "grid", None),
    )
    out_specs = (
        P("leaf", None, None, None, "grid", None),
        P("leaf", None, None, None, "grid", None),
    )
    return jax.shard_map(body, mesh=mesh, in_specs=in_specs, out_specs=out_specs, check_vma=False)
```

time: 1660 us -> 478 us (0.29)
  waiting for transfers between devices: 786 us -> 74 us
  other arithmetic: 500 us -> 2.96 us
  Pallas kernels: 0 us -> 348 us
  matrix products: 141 us -> 0 us
  between operations: 102 us -> 13.9 us
  local copies, waits for them, and re-layouts: 111 us -> 28.3 us
    psum x16 -> x0, waiting for transfers between devices: 706 us -> none  [broadcast(): return lax.psum(jnp.where(mine, value, jnp.zeros_like(value)), axis)]
    another operation x119 -> x0, other arithmetic: 410 us -> none  [the longest x48 211 us: panel_factor(): lower_part = jnp.linalg.cholesky(column_tail[:, :NB])]
    pallas_call x0 -> x4, Pallas kernels: none -> 348 us  [call(): pl.pallas_call(kernel, out_shape=outs, in_specs=[SMEM] * len(smem) + [VME...]
    dot_general x57 -> x0, matrix products: 109 us -> none  [the longest x48 72.9 us: apply_panel(): change = jnp.einsum('frn,fsn->frs', panel_cols, partner, precision=highest)]
    select_n x61 -> x1, other arithmetic: 57.7 us -> 0.01 us  [body(): first = jnp.where(member == 0, shifts, other_shifts)]
    unnamed x205 -> x12, local copies, waits for them, and re-layouts: 48.8 us -> 14.8 us
    another operation x16 -> x0, matrix products: 31.8 us -> none  [panel_factor(): lax.linalg.triangular_solve(lower_part, column_tail[:, NB:], left_side=Fa...]
    another operation x32 -> x0, local copies, waits for them, and re-layouts: 28.3 us -> none
  transfers between devices with their start and end apart: 26 -> 6, of which waited for: 17 -> 1; matrix products, arithmetic and copies ran while one was open for 7% -> 5% of each run, Pallas kernels for 0% -> 35%
where the time goes in v1:
time: 478 us; the launch traced here: 475 us
  Pallas kernels  348 us (73%)
  waiting for transfers between devices  74 us (15%)
  local copies, waits for them, and re-layouts  28.3 us (6%)
  between operations  13.9 us (3%)
  blocking collectives  8.15 us (2%)
    pallas_call x4, Pallas kernels, call(): pl.pallas_call(kernel, out_shape=outs, in_specs=[SMEM] * len(smem) + [VME...  348 us
    all_gather x4, waiting for transfers between devices, body(): lax.all_gather(entries[t * grid_count * NB:, t, :], 'grid', axis=0)  73.9 us
    unnamed x12, local copies, waits for them, and re-layouts  14.8 us
    slice x4, local copies, waits for them, and re-layouts, body(): entries[t * grid_count * NB:, t, :]  11.6 us
  transfers between devices with their start and end apart: 6, of which 1 were waited for; matrix products, arithmetic and copies ran while one was open for 5% of the time, Pallas kernels for 35%

profile of v1, /device:TPU:0, one launch (start us, length us, event | category | flops | bytes accessed | tf_op | source)
XLA Modules:
  0.0 475.1 jit_solution(14632891282456644504)
XLA Ops:
  7.2 0.0 copy-start
  7.2 0.0 all-gather.10.cloned.1.call-start
  7.2 3.4 slice.26
  10.6 0.0 all-gather.10.cloned.1.call-update
  10.6 0.0 all-gather.12.cloned.1.call-start
  10.7 3.0 slice.27
  13.7 0.0 all-gather.12.cloned.1.call-update
  13.8 0.0 all-gather.16.cloned.1.call-start
  13.8 2.2 slice.29
  16.0 0.0 all-gather.16.cloned.1.call-update
  16.0 0.0 all-gather.14.cloned.1.call-start
  16.1 3.0 slice.28
  19.0 0.0 all-gather.14.cloned.1.call-update
  19.1 1.3 constant_dynamic-slice_fusion
  20.4 73.9 %all-gather.10.cloned.1.call-done = f32[8192,1,128]{2,1,0:T(1,128)} async-done(((f32[2048,1,128]{2,1,0:T(1,128)}), f32[8192,1,128]{2,1,0:T(1,128)}) %all-gather.10.cloned.1.call-update) | async-done | bytes 4194320 | tf_op jit(solution)/shard_map/all_gather | solution.py:329
  94.3 82.2 %shard_map.68 = (f32[2048,128]{1,0:T(8,128)}, bf16[2,2048,256]{2,1,0:T(8,128)(2,1)}, bf16[2,2048,256]{2,1,0:T(8,128)(2,1)}) custom-call(s32[16]{0:T(128)} %bitcast.38, s32[1]{0:T(128)} %bitcast.1.place, f32[4,2048,128]{2,1,0:T(8,128)} %bitcast.42), custom_call_target="tpu_custom_call" | custom-call | flops 24999999488 | bytes 9437184 | tf_op jit(solution)/shard_map/pallas_call | solution.py:300
  176.4 0.0 all-gather.12.cloned.1.call-done
  176.4 85.8 %shard_map.69 = (f32[2048,128]{1,0:T(8,128)}, bf16[2,1536,256]{2,1,0:T(8,128)(2,1)}, bf16[2,1536,256]{2,1,0:T(8,128)(2,1)}) custom-call(s32[16]{0:T(128)} %bitcast.39, s32[1]{0:T(128)} %bitcast.1.place, f32[4,1536,128]{2,1,0:T(8,128)} %bitcast.43, bf16[2,2048,256]{2,1,0:T(8,128)(2,1)} %get-tuple-element.9.rest_0_.rest_2_, ...), custom_call_target="tpu_custom_call" | custom-call | flops 24999999488 | bytes 11534336 | tf_op jit(solution)/shard_map/pallas_call | solution.py:300
  262.2 0.0 all-gather.16.cloned.1.call-done
  262.2 0.0 all-gather.14.cloned.1.call-done
  262.2 0.0 copy-start.4
  262.2 0.0 copy-start.3
  262.2 0.0 copy-start.1
  262.2 0.0 copy-start.2
  262.3 12.4 %shard_map.70.mine = f32[8,1024,128]{2,1,0:T(8,128)} custom-call(s32[16]{0:T(128)} %bitcast.40, f32[4,1024,128]{2,1,0:T(8,128)} %bitcast.44, f32[4,512,128]{2,1,0:T(8,128)} %bitcast.45, bf16[2,2048,256]{2,1,0:T(8,128)(2,1)} %get-tuple-element.9.rest_0_.rest_2_, bf16[2,2048,256]{2,1,0:T(8,128)(2,1)} %get-tuple-element.10.rest_1_.rest_3_, ...), custom_call_target="tpu_custom_call" | custom-call | flops 6000000000 | bytes 14680064 | tf_op jit(solution)/shard_map/pallas_call | solution.py:300
  274.6 0.0 collective-permute-start
  274.7 0.0 copy-done.4
  274.7 8.1 %all-gather.4 = f32[4,1,2,1,128]{4,2,3,1,0:T(2,128)S(1)} all-gather(f32[1,1,2,1,128]{4,2,3,1,0:T(2,128)S(1)} %bitcast.41), channel_id=6, replica_groups=mesh['leaf'=8,'grid'=4] {'grid'}, dimensions={0}, use_global_device_ids=true | all-gather | bytes 5120 | tf_op jit(solution)/shard_map/all_gather | solution.py:327
  282.8 0.0 collective-permute-start.1
  282.8 0.0 copy-done
  282.8 0.7 fusion.4
  283.5 0.0 copy-done.3
  283.5 0.1 compare_bitcast_fusion
  283.6 0.1 select_reduce_fusion.1
  283.7 0.6 broadcast_add_fusion.1.mine_at
  284.2 0.5 broadcast_add_fusion.other_at
  284.8 0.1 iota_compare_fusion
  284.8 0.8 fusion.2.blocks
  285.6 0.0 collective-permute-done.1
  285.6 0.7 select_reduce_fusion.diagonal
  286.4 0.0 copy-done.1
  286.4 0.0 copy-done.2
  286.4 0.1 maximum_bitcast_fusion
  286.5 10.0 %copy.13 = f32[1,1,2048,2,1,128]{5,4,3,2,1,0:T(1,128)} copy(f32[1,1,2048,2,1,128]{5,2,3,4,1,0:T(8,128)S(1)} %maximum_bitcast_fusion) | data formatting | bytes 4194304
  296.5 0.0 collective-permute-done.other
  296.5 167.3 %shard_map.71 = f32[2,2048,128]{2,1,0:T(8,128)} custom-call(s32[2]{0:T(128)} %fusion.2.blocks, s32[16]{0:T(128)} %broadcast_add_fusion.1.mine_at, s32[16]{0:T(128)} %broadcast_add_fusion.other_at, f32[8,1024,128]{2,1,0:T(8,128)} %shard_map.70.mine, f32[8,1024,128]{2,1,0:T(8,128)} %collective-permute-done.other, f32[16,128]{1,0:T(8,128)} %select_reduce_fusion.diagonal), custom_call_target="tpu_custom_call" | custom-call | flops 49999998976 | bytes 10493952 | tf_op jit(solution)/shard_map/pallas_call | solution.py:300
  463.8 4.8 %copy.14 = f32[1,1,2048,2,1,128]{5,4,3,2,1,0:T(1,128)} copy(f32[1,1,2048,2,1,128]{5,2,3,4,1,0:T(8,128)} %bitcast.29) | data formatting | bytes 4194304
  (5 shorter events, 0.0 us)
Async XLA Ops:
  7.2 275.7 %copy-start = (s32[4,16]{1,0:T(4,128)S(1)}, s32[4,16]{1,0:T(4,128)}, u32[]{:S(2)}) copy-start(s32[4,16]{1,0:T(4,128)} %param.8) | copy-start | bytes 772
  7.2 87.1 %all-gather.10.cloned.1.call-start = ((), (), s32[]{:S(2)}) async-start(), calls=%async_computation | async-start | bytes 5242880 | tf_op jit(solution)/shard_map/all_gather | solution.py:329
  10.6 165.8 %all-gather.12.cloned.1.call-start = ((), (), s32[]{:S(2)}) async-start(), calls=%async_computation.1 | async-start | bytes 3932160 | tf_op jit(solution)/shard_map/all_gather | solution.py:329
  13.8 248.5 %all-gather.16.cloned.1.call-start = ((), (), s32[]{:S(2)}) async-start(), calls=%async_computation.3 | async-start | bytes 1310720 | tf_op jit(solution)/shard_map/all_gather | solution.py:329
  16.0 246.2 %all-gather.14.cloned.1.call-start = ((), (), s32[]{:S(2)}) async-start(), calls=%async_computation.2 | async-start | bytes 2621440 | tf_op jit(solution)/shard_map/all_gather | solution.py:329
  262.2 12.4 %copy-start.4 = (f32[1,1,2,1,128]{4,3,2,1,0:T(1,128)S(1)}, f32[1,1,2,1,128]{4,3,2,1,0:T(1,128)}, u32[]{:S(2)}) copy-start(f32[1,1,2,1,128]{4,3,2,1,0:T(1,128)} %param.9) | copy-start | bytes 3076
  262.2 21.3 %copy-start.3 = (s32[1,1,16]{2,1,0:T(1,128)S(1)}, s32[1,1,16]{2,1,0:T(1,128)}, u32[]{:S(2)}) copy-start(s32[1,1,16]{2,1,0:T(1,128)} %get-tuple-element.27) | copy-start | bytes 196
  262.2 24.1 %copy-start.1 = (f32[2048,128]{1,0:T(8,128)S(1)}, f32[2048,128]{1,0:T(8,128)}, u32[]{:S(2)}) copy-start(f32[2048,128]{1,0:T(8,128)} %get-tuple-element.8) | copy-start | bytes 3145732
  262.2 24.1 %copy-start.2 = (f32[2048,128]{1,0:T(8,128)S(1)}, f32[2048,128]{1,0:T(8,128)}, u32[]{:S(2)}) copy-start(f32[2048,128]{1,0:T(8,128)} %get-tuple-element.11) | copy-start | bytes 3145732
  274.6 21.8 %collective-permute-start = (f32[8,1024,128]{2,1,0:T(8,128)}, f32[8,1024,128]{2,1,0:T(8,128)}, u32[]{:S(2)}, u32[]{:S(2)}) collective-permute-start(f32[8,1024,128]{2,1,0:T(8,128)} %shard_map.70.mine), channel_id=1, source_target_pairs={{0,4},{4,0},{8,12},{12,8},{16,20},{20,16},{24,28},{28,24},{1,5},{5... | collective-permute-start | bytes 12582920 | tf_op jit(solution)/shard_map/ppermute | solution.py:376
  282.8 2.8 collective-permute-start.1
Sparse Core Ops, SparseCore 0:
  10.8 83.4 all-gather.9
  95.8 62.1 all-gather.11
  159.5 26.4 all-gather.15
  187.5 45.3 all-gather.13

commit v2 on v1

--- a/solution.py
+++ b/solution.py
@@ -45,24 +45,32 @@
     groups = NB // 8
     left = [block_ref[8 * g : 8 * g + 8, :] for g in range(groups)]
     right = [jnp.where(lane == sub + 8 * g, 1.0, 0.0).astype(f32) for g in range(groups)]
-    for step in range(NB):
-        g, j = divmod(step, 8)
-        column = jnp.broadcast_to(left[g][:, step : step + 1], (8, NB))
-        pivot = jnp.broadcast_to(column[j : j + 1, :], (8, NB))
-        scale = 1.0 / pivot
-        row_left = jnp.broadcast_to(left[g][j : j + 1, :], (8, NB)) * scale
-        row_right = jnp.broadcast_to(right[g][j : j + 1, :], (8, NB)) * scale
-        diagonal = pivot if j == 0 else jnp.where(sub >= j, pivot, diagonal)
-        if j < 7:
-            below = jnp.where(sub > j, column, 0.0)
-            left[g] = left[g] - below * row_left
-            right[g] = right[g] - below * row_right
+    for g in range(groups):
+        columns = [jnp.broadcast_to(left[g][:, 8 * g + i : 8 * g + i + 1], (8, NB)) for i in range(8)]
+        rows_left, rows_right = left[g], right[g]
+        diagonal = solved = None
+        for i in range(8):
+            pivot = jnp.broadcast_to(columns[i][i : i + 1, :], (8, NB))
+            factor = jnp.where(sub == i, 0.0, columns[i]) * (1.0 / pivot)
+            for c in range(i + 1, 8):
+                columns[c] = columns[c] - factor * jnp.broadcast_to(columns[c][i : i + 1, :], (8, NB))
+            row_right = jnp.broadcast_to(rows_right[i : i + 1, :], (8, NB))
+            diagonal = pivot if i == 0 else jnp.where(sub == i, pivot, diagonal)
+            solved = row_right if i == 0 else jnp.where(sub == i, row_right, solved)
+            rows_left = rows_left - factor * jnp.broadcast_to(rows_left[i : i + 1, :], (8, NB))
+            rows_right = rows_right - factor * row_right
+        inverse_ref[8 * g : 8 * g + 8, :] = solved * lax.rsqrt(diagonal)
+        if g + 1 == groups:
+            break
+        over = 1.0 / diagonal
+        rows_left, rows_right = rows_left * over, rows_right * over
+        spread_left = [jnp.broadcast_to(rows_left[i : i + 1, :], (8, NB)) for i in range(8)]
+        spread_right = [jnp.broadcast_to(rows_right[i : i + 1, :], (8, NB)) for i in range(8)]
         for v in range(g + 1, groups):
-            column = jnp.broadcast_to(left[v][:, step : step + 1], (8, NB))
-            left[v] = left[v] - column * row_left
-            right[v] = right[v] - column * row_right
-        if j == 7:
-            inverse_ref[8 * g : 8 * g + 8, :] = right[g] * lax.rsqrt(diagonal)
+            factors = [jnp.broadcast_to(left[v][:, 8 * g + i : 8 * g + i + 1], (8, NB)) for i in range(8)]
+            for i in range(8):
+                left[v] = left[v] - factors[i] * spread_left[i]
+                right[v] = right[v] - factors[i] * spread_right[i]
 
 
 def factor_blocks(front, high, low, block, inverse, count, height, emit):
@@ -349,6 +357,7 @@
     chosen = owner_row[:, None, None] == jnp.arange(FB)[None, :, None]
     diagonal = jnp.sum(jnp.where(chosen, by_slot[None], 0.0), axis=1)
 
+    gathered[0], diagonal = lax.optimization_barrier((gathered[0], diagonal))
     place = grid_pos.astype(jnp.int32).reshape(1)
     owned = []
     done = []

time: 478 us -> 338 us (0.71)
  Pallas kernels: 348 us -> 145 us
  waiting for transfers between devices: 74 us -> 134 us
    pallas_call x4, Pallas kernels: 348 us -> 145 us  [call(): pl.pallas_call(kernel, out_shape=outs, in_specs=[SMEM] * len(smem) + [VME...]
    all_gather x4, waiting for transfers between devices: 73.9 us -> 134 us  [body(): lax.all_gather(entries[t * grid_count * NB:, t, :], 'grid', axis=0)]
  transfers between devices with their start and end apart: 6 -> 6, of which waited for: 1 -> 3; matrix products, arithmetic and copies ran while one was open for 5% -> 7% of each run, Pallas kernels for 35% -> 19%
where the time goes in v2:
time: 338 us; the launch traced here: 337 us
  Pallas kernels  145 us (43%)
  waiting for transfers between devices  134 us (40%)
  local copies, waits for them, and re-layouts  28.5 us (8%)
  between operations  13.9 us (4%)
  blocking collectives  12.7 us (4%)
    pallas_call x4, Pallas kernels, call(): pl.pallas_call(kernel, out_shape=outs, in_specs=[SMEM] * len(smem) + [VME...  145 us
    all_gather x4, waiting for transfers between devices, body(): lax.all_gather(entries[t * grid_count * NB:, t, :], 'grid', axis=0)  134 us
    unnamed x12, local copies, waits for them, and re-layouts  15 us
    all_gather x1, blocking collectives, body(): shifts = lax.all_gather(parent_shift.reshape(slots, NB), 'grid', axis=0)  12.7 us
    slice x4, local copies, waits for them, and re-layouts, body(): entries[t * grid_count * NB:, t, :]  11.6 us
  transfers between devices with their start and end apart: 6, of which 3 were waited for; matrix products, arithmetic and copies ran while one was open for 7% of the time, Pallas kernels for 19%

profile of v2, /device:TPU:0, one launch (start us, length us, event | category | flops | bytes accessed | tf_op | source)
XLA Modules:
  0.0 337.1 jit_solution(7973561091916013625)
XLA Ops:
  7.2 0.0 copy-start
  7.2 0.0 all-gather.10.cloned.1.call-start
  7.2 3.4 %slice.26 = f32[2048,1,128]{2,1,0:T(1,128)} slice(f32[2048,4,128]{2,1,0:T(4,128)} %bitcast.30), slice={[0:2048], [0:1], [0:128]} | slice | bytes 2097152 | tf_op jit(solution)/shard_map/slice | solution.py:337
  10.6 0.0 copy-start.4
  10.6 0.0 all-gather.10.cloned.1.call-update
  10.6 0.0 all-gather.12.cloned.1.call-start
  10.7 3.1 slice.27
  13.7 0.0 all-gather.12.cloned.1.call-update
  13.8 0.0 all-gather.16.cloned.1.call-start
  13.8 2.2 slice.29
  16.0 0.0 all-gather.16.cloned.1.call-update
  16.0 0.0 all-gather.14.cloned.1.call-start
  16.1 0.0 copy-done.4
  16.1 12.7 %all-gather.1 = f32[4,1,2,1,128]{4,2,3,1,0:T(2,128)S(1)} all-gather(f32[1,1,2,1,128]{4,2,3,1,0:T(2,128)S(1)} %bitcast.41), channel_id=3, replica_groups=mesh['leaf'=8,'grid'=4] {'grid'}, dimensions={0}, use_global_device_ids=true | all-gather | bytes 5120 | tf_op jit(solution)/shard_map/all_gather | solution.py:335
  28.8 0.0 collective-permute-start
  28.8 3.0 slice.28
  31.8 0.0 all-gather.14.cloned.1.call-update
  31.8 0.0 copy-done
  31.9 0.1 iota_compare_fusion
  31.9 1.2 constant_dynamic-slice_fusion
  33.2 0.0 collective-permute-done
  33.2 0.7 select_reduce_fusion.diagonal
  33.9 60.3 %all-gather.10.cloned.1.call-done = f32[8192,1,128]{2,1,0:T(1,128)} async-done(((f32[2048,1,128]{2,1,0:T(1,128)}), f32[8192,1,128]{2,1,0:T(1,128)}) %all-gather.10.cloned.1.call-update) | async-done | bytes 4194320 | tf_op jit(solution)/shard_map/all_gather | solution.py:337
  94.2 31.0 %shard_map.68 = (f32[2048,128]{1,0:T(8,128)}, bf16[2,2048,256]{2,1,0:T(8,128)(2,1)}, bf16[2,2048,256]{2,1,0:T(8,128)(2,1)}) custom-call(s32[16]{0:T(128)} %bitcast.38, s32[1]{0:T(128)} %bitcast.1.place, f32[4,2048,128]{2,1,0:T(8,128)} %bitcast.42), custom_call_target="tpu_custom_call" | custom-call | flops 24999999488 | bytes 9437184 | tf_op jit(solution)/shard_map/pallas_call | solution.py:308
  125.2 32.7 %all-gather.12.cloned.1.call-done = f32[6144,1,128]{2,1,0:T(1,128)} async-done(((f32[1536,1,128]{2,1,0:T(1,128)}), f32[6144,1,128]{2,1,0:T(1,128)}) %all-gather.12.cloned.1.call-update) | async-done | bytes 3145744 | tf_op jit(solution)/shard_map/all_gather | solution.py:337
  157.9 34.5 %shard_map.69 = (f32[2048,128]{1,0:T(8,128)}, bf16[2,1536,256]{2,1,0:T(8,128)(2,1)}, bf16[2,1536,256]{2,1,0:T(8,128)(2,1)}) custom-call(s32[16]{0:T(128)} %bitcast.39, s32[1]{0:T(128)} %bitcast.1.place, f32[4,1536,128]{2,1,0:T(8,128)} %bitcast.43, bf16[2,2048,256]{2,1,0:T(8,128)(2,1)} %get-tuple-element.12.rest_0_.rest_2_, ...), custom_call_target="tpu_custom_call" | custom-call | flops 24999999488 | bytes 11534336 | tf_op jit(solution)/shard_map/pallas_call | solution.py:308
  192.4 0.0 all-gather.16.cloned.1.call-done
  192.4 40.6 %all-gather.14.cloned.1.call-done = f32[4096,1,128]{2,1,0:T(1,128)} async-done(((f32[1024,1,128]{2,1,0:T(1,128)}), f32[4096,1,128]{2,1,0:T(1,128)}) %all-gather.14.cloned.1.call-update) | async-done | bytes 2097168 | tf_op jit(solution)/shard_map/all_gather | solution.py:337
  233.0 0.0 copy-start.3
  233.0 0.0 copy-start.1
  233.0 0.0 copy-start.2
  233.0 12.2 %shard_map.70.mine = f32[8,1024,128]{2,1,0:T(8,128)} custom-call(s32[16]{0:T(128)} %bitcast.40, f32[4,1024,128]{2,1,0:T(8,128)} %bitcast.44, f32[4,512,128]{2,1,0:T(8,128)} %bitcast.45, bf16[2,2048,256]{2,1,0:T(8,128)(2,1)} %get-tuple-element.12.rest_0_.rest_2_, bf16[2,2048,256]{2,1,0:T(8,128)(2,1)} %get-tuple-element.13.rest_1_.rest_3_, ...), custom_call_target="tpu_custom_call" | custom-call | flops 6000000000 | bytes 14680064 | tf_op jit(solution)/shard_map/pallas_call | solution.py:308
  245.3 0.0 collective-permute-start.1
  245.3 0.7 fusion.4
  246.0 0.7 fusion.2.blocks
  246.7 0.0 copy-done.3
  246.7 0.1 compare_bitcast_fusion
  246.7 0.1 select_reduce_fusion.1
  246.8 0.5 broadcast_add_fusion.other_at
  247.4 0.5 broadcast_add_fusion.1.mine_at
  247.9 0.0 copy-done.1
  247.9 0.0 copy-done.2
  247.9 0.1 maximum_bitcast_fusion
  248.1 10.2 %copy.13 = f32[1,1,2048,2,1,128]{5,4,3,2,1,0:T(1,128)} copy(f32[1,1,2048,2,1,128]{5,2,3,4,1,0:T(8,128)S(1)} %maximum_bitcast_fusion) | data formatting | bytes 4194304
  258.2 0.0 collective-permute-done.1.other
  258.2 67.6 %shard_map.71 = f32[2,2048,128]{2,1,0:T(8,128)} custom-call(s32[2]{0:T(128)} %fusion.2.blocks, s32[16]{0:T(128)} %broadcast_add_fusion.1.mine_at, s32[16]{0:T(128)} %broadcast_add_fusion.other_at, f32[8,1024,128]{2,1,0:T(8,128)} %shard_map.70.mine, f32[8,1024,128]{2,1,0:T(8,128)} %collective-permute-done.1.other, f32[16,128]{1,0:T(8,128)} %select_reduce_fusion.diagonal), custom_call_target="tpu_custom_call" | custom-call | flops 49999998976 | bytes 10493952 | tf_op jit(solution)/shard_map/pallas_call | solution.py:308
  325.8 4.8 %copy.14 = f32[1,1,2048,2,1,128]{5,4,3,2,1,0:T(1,128)} copy(f32[1,1,2048,2,1,128]{5,2,3,4,1,0:T(8,128)} %bitcast.29) | data formatting | bytes 4194304
  (5 shorter events, 0.0 us)
Async XLA Ops:
  7.2 24.7 %copy-start = (s32[4,16]{1,0:T(4,128)S(1)}, s32[4,16]{1,0:T(4,128)}, u32[]{:S(2)}) copy-start(s32[4,16]{1,0:T(4,128)} %param.8) | copy-start | bytes 772
  7.2 87.1 %all-gather.10.cloned.1.call-start = ((), (), s32[]{:S(2)}) async-start(), calls=%async_computation | async-start | bytes 5242880 | tf_op jit(solution)/shard_map/all_gather | solution.py:337
  10.6 5.5 %copy-start.4 = (f32[1,1,2,1,128]{4,3,2,1,0:T(1,128)S(1)}, f32[1,1,2,1,128]{4,3,2,1,0:T(1,128)}, u32[]{:S(2)}) copy-start(f32[1,1,2,1,128]{4,3,2,1,0:T(1,128)} %param.9) | copy-start | bytes 3076
  10.6 147.3 %all-gather.12.cloned.1.call-start = ((), (), s32[]{:S(2)}) async-start(), calls=%async_computation.1 | async-start | bytes 3932160 | tf_op jit(solution)/shard_map/all_gather | solution.py:337
  13.8 178.6 %all-gather.16.cloned.1.call-start = ((), (), s32[]{:S(2)}) async-start(), calls=%async_computation.3 | async-start | bytes 1310720 | tf_op jit(solution)/shard_map/all_gather | solution.py:337
  16.0 217.0 %all-gather.14.cloned.1.call-start = ((), (), s32[]{:S(2)}) async-start(), calls=%async_computation.2 | async-start | bytes 2621440 | tf_op jit(solution)/shard_map/all_gather | solution.py:337
  28.8 4.4 %collective-permute-start = (f32[4,2,128]{2,1,0:T(2,128)S(1)}, f32[4,2,128]{2,1,0:T(2,128)S(1)}, u32[]{:S(2)}, u32[]{:S(2)}) collective-permute-start(f32[4,2,128]{2,1,0:T(2,128)S(1)} %bitcast.37), channel_id=1, source_target_pairs={{0,4},{4,0},{8,12},{12,8},{16,20},{20,16},{24,28},{28,24},{1,5},{5... | collective-permute-start | bytes 12296 | tf_op jit(solution)/shard_map/ppermute | solution.py:353
  233.0 13.6 %copy-start.3 = (s32[1,1,16]{2,1,0:T(1,128)S(1)}, s32[1,1,16]{2,1,0:T(1,128)}, u32[]{:S(2)}) copy-start(s32[1,1,16]{2,1,0:T(1,128)} %get-tuple-element.31) | copy-start | bytes 196
  233.0 14.9 %copy-start.1 = (f32[2048,128]{1,0:T(8,128)S(1)}, f32[2048,128]{1,0:T(8,128)}, u32[]{:S(2)}) copy-start(f32[2048,128]{1,0:T(8,128)} %get-tuple-element.11) | copy-start | bytes 3145732
  233.0 14.9 %copy-start.2 = (f32[2048,128]{1,0:T(8,128)S(1)}, f32[2048,128]{1,0:T(8,128)}, u32[]{:S(2)}) copy-start(f32[2048,128]{1,0:T(8,128)} %get-tuple-element.14) | copy-start | bytes 3145732
  245.3 12.9 %collective-permute-start.1 = (f32[8,1024,128]{2,1,0:T(8,128)}, f32[8,1024,128]{2,1,0:T(8,128)}, u32[]{:S(2)}, u32[]{:S(2)}) collective-permute-start(f32[8,1024,128]{2,1,0:T(8,128)} %shard_map.70.mine), channel_id=1, source_target_pairs={{0,4},{4,0},{8,12},{12,8},{16,20},{20,16},{24,28},{28,24},{1,5},{5... | collective-permute-start | bytes 12582920 | tf_op jit(solution)/shard_map/ppermute | solution.py:385
Sparse Core Ops, SparseCore 0:
  10.8 83.4 all-gather.9
  95.8 62.0 all-gather.11
  159.5 26.6 all-gather.15
  187.6 45.4 all-gather.13

commit v3 on v2

--- a/solution.py
+++ b/solution.py
@@ -142,11 +142,29 @@
     lax.fori_loop(0, count, step, 0)
 
 
+def entry_block(entries, grid_count, row, col):
+    most = grid_count // 2
+    if row >= grid_count:
+        at = most + 1 + row - grid_count
+        return entries[col, at * NB : (at + 1) * NB, :]
+    at = row - col
+    if at <= most:
+        return entries[col, at * NB : (at + 1) * NB, :]
+    at = grid_count - at
+    return entries[row, at * NB : (at + 1) * NB, :].T
+
+
+def packed_at(row, col):
+    return col * CB - col * (col - 1) // 2 + row - col
+
+
 def masked(value, live_row, live_col, same):
+    if not same:
+        return jnp.where(live_row * live_col > 0, value, 0.0)
     row = lax.broadcasted_iota(jnp.int32, (NB, NB), 0)
     col = lax.broadcasted_iota(jnp.int32, (NB, NB), 1)
     kept = jnp.where(live_row * live_col > 0, value, 0.0)
-    alone = jnp.where(same & (live_row == 0), 1.0, 0.0)
+    alone = jnp.where(live_row == 0, 1.0, 0.0)
     return kept + jnp.where(row == col, alone, 0.0)
 
 
@@ -157,17 +175,12 @@
     height = F - base
     own[...] = jnp.zeros_like(own)
 
-    def load(q, carry):
-        for half in range(2):
-            col = 2 * q + half
-            live_col = live[index * grid_count + col]
-            for r in range(height // NB):
-                front[q, r * NB : (r + 1) * NB, half * NB : (half + 1) * NB] = masked(
-                    entries[col, r * NB : (r + 1) * NB, :], live[base // NB + r], live_col, col == r
-                )
-        return carry
-
-    lax.fori_loop(0, grid_count // 2, load, 0)
+    for col in range(grid_count):
+        live_col = live[index * grid_count + col]
+        for r in range(col, height // NB):
+            front[col // 2, r * NB : (r + 1) * NB, col % 2 * NB : (col % 2 + 1) * NB] = masked(
+                entry_block(entries, grid_count, r, col), live[base // NB + r], live_col, col == r
+            )
     for earlier in range(index):
         past_high, past_low = done[2 * earlier], done[2 * earlier + 1]
         offset = (index - earlier) * grid_count * NB
@@ -198,15 +211,10 @@
     factor_blocks(front, high, low, block, inverse, grid_count, height, emit)
 
 
-def schur_kernel(rounds, pivot_rounds, grid_count, live, *rest):
-    late = rounds - pivot_rounds
-    entries = rest[:late]
-    done = rest[late : late + 2 * pivot_rounds]
-    (out,) = rest[late + 2 * pivot_rounds :]
+def product_kernel(pivot_rounds, grid_count, *rest):
+    done = rest[: 2 * pivot_rounds]
+    (out,) = rest[2 * pivot_rounds :]
     for q in range(CB // 2):
-        source = 2 * q // grid_count
-        inner = 2 * q % grid_count
-        shift = source * grid_count * NB
 
         def tile(k, carry):
             total = None
@@ -224,16 +232,27 @@
                 for col in range(2):
                     r = 2 * k + row
                     c = 2 * q + col
-                    value = entries[source][inner + col, pl.ds(pl.multiple_of(r * NB - shift, NB), NB), :]
-                    value = masked(value, live[PB + r], live[PB + c], r == c)
-                    part = total[row * NB : (row + 1) * NB, col * NB : (col + 1) * NB]
-                    out[c, rows_of(r, NB), :] = value - part
+
+                    @pl.when(r >= c)
+                    def _():
+                        part = total[row * NB : (row + 1) * NB, col * NB : (col + 1) * NB]
+                        out[packed_at(r, c)] = part
+
             return carry
 
         lax.fori_loop(q, CB // 2, tile, 0)
 
 
-def parent_kernel(slots, blocks, mine_at, other_at, mine, other, diagonal, own, front, high, low, block, inverse):
+def parent_kernel(slots, grid_count, late, blocks, mine_at, other_at, *rest):
+    my_entries, other_entries = rest[:late], rest[late : 2 * late]
+    my_product, other_product, diagonal, out = rest[2 * late : 2 * late + 4]
+    mine, other, own, front, high, low, block, inverse, sems = rest[2 * late + 4 :]
+    for schur, entries, product in ((mine, my_entries, my_product), (other, other_entries, other_product)):
+        for c in range(CB):
+            t, inner = divmod(c, grid_count)
+            for r in range(c, CB):
+                at = packed_at(r, c)
+                schur[at] = entry_block(entries[t], grid_count, r - t * grid_count, inner) - product[at]
     row_id = lax.broadcasted_iota(jnp.int32, (NB, NB), 0)
     col_id = lax.broadcasted_iota(jnp.int32, (NB, NB), 1)
     own[...] = jnp.zeros_like(own)
@@ -241,11 +260,11 @@
     def extension(schur, at, r, b, turn):
         cr, cb = at[r], at[b]
         present = (cr >= 0) & (cb >= 0)
-        cr, cb = jnp.maximum(cr, 0), jnp.maximum(cb, 0)
+        cr, cb = jnp.where(present, cr, 0), jnp.where(present, cb, 0)
         if not turn:
-            value = schur[cb, rows_of(cr, NB), :]
+            value = schur[packed_at(cr, cb)]
         else:
-            value = schur[jnp.minimum(cr, cb), rows_of(jnp.maximum(cr, cb), NB), :]
+            value = schur[packed_at(jnp.maximum(cr, cb), jnp.minimum(cr, cb))]
             value = jnp.where(cr >= cb, value, value.T)
         return jnp.where(present, value, 0.0)
 
@@ -301,15 +320,20 @@
         return carry
 
     lax.fori_loop(0, slots, finish, 0)
-
-
-def call(kernel, outs, scratch, smem, vmem, flops):
+    copies = [pltpu.make_async_copy(own.at[s], out.at[:, s, 0, :], sems.at[s]) for s in range(slots)]
+    for copy in copies:
+        copy.start()
+    for copy in copies:
+        copy.wait()
+
+
+def call(kernel, outs, scratch, smem, vmem, flops, out_space=pltpu.VMEM):
     size = sum(a.size * a.dtype.itemsize for a in vmem) + sum(a.size * a.dtype.itemsize for a in outs)
     return pl.pallas_call(
         kernel,
         out_shape=outs,
         in_specs=[SMEM] * len(smem) + [VMEM] * len(vmem),
-        out_specs=[VMEM] * len(outs),
+        out_specs=[pl.BlockSpec(memory_space=out_space)] * len(outs),
         scratch_shapes=scratch,
         compiler_params=pltpu.CompilerParams(vmem_limit_bytes=LIMIT),
         cost_estimate=pl.CostEstimate(flops=flops, bytes_accessed=size, transcendentals=0),
@@ -333,9 +357,15 @@
     swap = [(source, source ^ 1) for source in range(leaf_count)]
     entries = child_front.reshape(F, rounds, NB)
     shifts = lax.all_gather(parent_shift.reshape(slots, NB), "grid", axis=0)
-    gathered = [
-        lax.all_gather(entries[t * grid_count * NB :, t, :], "grid", axis=0) for t in range(rounds)
-    ]
+    half_ring = (grid_pos + jnp.arange(grid_count // 2 + 1)) % grid_count
+
+    def sent(t):
+        base = t * grid_count * NB
+        near = entries[base : base + grid_count * NB, t, :].reshape(grid_count, NB, NB)
+        near = jnp.take(near, half_ring, axis=0).reshape(-1, NB)
+        return jnp.concatenate([near, entries[base + grid_count * NB :, t, :]], axis=0)
+
+    gathered = [lax.all_gather(sent(t), "grid", axis=0) for t in range(rounds)]
 
     my_live = lax.dynamic_index_in_dim(child_live, leaf_pos, 0, keepdims=False)[0]
     other_live = lax.dynamic_index_in_dim(child_live, sibling, 0, keepdims=False)[0]
@@ -374,35 +404,42 @@
         )
         owned.append(own)
         done += [high, low]
+    late = gathered[pivot_rounds:]
+    lower = CB * (CB + 1) // 2
     (mine,) = call(
-        functools.partial(schur_kernel, rounds, pivot_rounds, grid_count),
-        [shape((CB, F - PIVOTS, NB))],
+        functools.partial(product_kernel, pivot_rounds, grid_count),
+        [shape((lower, NB, NB))],
         [],
-        [my_live],
-        [*gathered[pivot_rounds:], *done],
+        [],
+        done,
         6_000_000_000,
     )
     other = lax.ppermute(mine, "leaf", swap)
+    other_late = [lax.ppermute(part, "leaf", swap) for part in late]
     packed = (PB // 2, F, PAIR)
     (parent,) = call(
-        functools.partial(parent_kernel, slots),
-        [shape((slots, F, NB))],
+        functools.partial(parent_kernel, slots, grid_count, len(late)),
+        [shape((F, slots, 1, NB))],
         [
+            pltpu.VMEM((lower, NB, NB), f32),
+            pltpu.VMEM((lower, NB, NB), f32),
+            pltpu.VMEM((slots, F, NB), f32),
             pltpu.VMEM(packed, f32),
             pltpu.VMEM(packed, bf16),
             pltpu.VMEM(packed, bf16),
             pltpu.VMEM((NB, NB), f32),
             pltpu.VMEM((NB, NB), f32),
+            pltpu.SemaphoreType.DMA((slots,)),
         ],
         [parent_blocks, sources(my_map, my_live), sources(other_map, other_live)],
-        [mine, other, diagonal],
+        [*late, *other_late, mine, other, diagonal],
         50_000_000_000,
+        pl.ANY,
     )
     child_factor = jnp.stack(owned, axis=1)
-    parent_done = jnp.swapaxes(parent, 0, 1)
     return (
         child_factor.reshape(1, 1, F, pivot_rounds, 1, NB),
-        parent_done.reshape(1, 1, F, slots, 1, NB),
+        parent.reshape(1, 1, F, slots, 1, NB),
     )
 
 

time: 338 us -> 308 us (0.911)
  waiting for transfers between devices: 134 us -> 88.9 us
  blocking collectives: 12.7 us -> 30.8 us
  local copies, waits for them, and re-layouts: 28.5 us -> 22.3 us
    all_gather x4 -> x3, waiting for transfers between devices: 134 us -> 88.8 us  [body(): gathered = [lax.all_gather(sent(t), 'grid', axis=0) for t in range(rounds)]]
    all_gather x0 -> x1, blocking collectives: none -> 17.9 us  [body(): gathered = [lax.all_gather(sent(t), 'grid', axis=0) for t in range(rounds)]]
    unnamed x12 -> x13, local copies, waits for them, and re-layouts: 15 us -> 10 us
    slice x4 -> x3, local copies, waits for them, and re-layouts: 11.6 us -> 8.09 us  [the longest x2 4.31 us: sent(): entries[base + grid_count * NB:, t, :]]
  transfers between devices with their start and end apart: 6 -> 7, of which waited for: 3 -> 2; matrix products, arithmetic and copies ran while one was open for 7% -> 6% of each run, Pallas kernels for 19% -> 25%
where the time goes in v3:
time: 308 us; the launch traced here: 305 us
  Pallas kernels  143 us (46%)
  waiting for transfers between devices  88.9 us (29%)
  blocking collectives  30.8 us (10%)
  local copies, waits for them, and re-layouts  22.3 us (7%)
  between operations  13.9 us (5%)
  other arithmetic  5.88 us (2%)
    pallas_call x4, Pallas kernels, call(): pl.pallas_call(kernel, out_shape=outs, in_specs=[SMEM] * len(smem) + [VME...  143 us
    all_gather x3, waiting for transfers between devices, body(): gathered = [lax.all_gather(sent(t), 'grid', axis=0) for t in range(rounds)]  88.8 us
    all_gather x1, blocking collectives, body(): gathered = [lax.all_gather(sent(t), 'grid', axis=0) for t in range(rounds)]  17.9 us
    all_gather x1, blocking collectives, body(): shifts = lax.all_gather(parent_shift.reshape(slots, NB), 'grid', axis=0)  12.9 us
    unnamed x13, local copies, waits for them, and re-layouts  10 us
  transfers between devices with their start and end apart: 7, of which 2 were waited for; matrix products, arithmetic and copies ran while one was open for 6% of the time, Pallas kernels for 25%

profile of v3, /device:TPU:0, one launch (start us, length us, event | category | flops | bytes accessed | tf_op | source)
XLA Modules:
  0.0 305.3 jit_solution(4296411369930224509)
XLA Ops:
  7.2 0.0 copy-start
  7.2 0.0 all-gather.8.cloned.1.call-start
  7.3 3.8 %fusion.7 = (f32[512,1,128]{2,1,0:T(1,128)S(1)}, f32[512,1,128]{2,1,0:T(1,128)S(1)}, f32[512,1,128]{2,1,0:T(1,128)S(1)}, f32[512,1,128]{2,1,0:T(1,128)S(1)}, f32[512,1,128]{2,1,0:T(1,128)S(1)}) fusion(f32[2048,4,128]{2,1,0:T(4,128)} %bitcast.41), kind=kLoop, calls=%fused_computation.46 | loop fusion | bytes 2621440 | tf_op jit(solution)/shard_map/slice | solution.py:364
  11.0 2.2 slice.47
  13.2 0.6 gather_fusion
  13.8 0.6 gather_fusion.1
  14.4 0.6 gather_fusion.2
  14.9 0.6 gather_fusion.3
  15.5 0.1 broadcast_select_fusion
  15.7 1.0 pad_maximum_fusion
  16.7 0.0 copy-start.5
  16.7 0.0 all-gather.8.cloned.1.call-update
  16.7 0.0 all-gather.10.cloned.1.call-start
  16.7 2.1 slice.49
  18.9 1.0 pad_maximum_fusion.1
  19.9 0.0 all-gather.10.cloned.1.call-update
  19.9 0.0 all-gather.12.cloned.1.call-start
  19.9 0.0 copy-done.5
  20.0 12.9 %all-gather.1 = f32[4,1,2,1,128]{4,2,3,1,0:T(2,128)S(1)} all-gather(f32[1,1,2,1,128]{4,2,3,1,0:T(2,128)S(1)} %bitcast.59), channel_id=3, replica_groups=mesh['leaf'=8,'grid'=4] {'grid'}, dimensions={0}, use_global_device_ids=true | all-gather | bytes 5120 | tf_op jit(solution)/shard_map/all_gather | solution.py:359
  32.9 0.0 collective-permute-start
  32.9 0.8 pad_maximum_fusion.2
  33.7 0.0 all-gather.12.cloned.1.call-update
  33.7 0.0 copy-done
  33.8 0.1 iota_compare_fusion
  33.8 1.2 constant_dynamic-slice_fusion
  35.1 0.0 collective-permute-done
  35.1 0.7 select_reduce_fusion.rest_6_
  35.8 60.2 %all-gather.8.cloned.1.call-done = f32[7680,128]{1,0:T(8,128)} async-done(((f32[1920,128]{1,0:T(8,128)}), f32[7680,128]{1,0:T(8,128)}) %all-gather.8.cloned.1.call-update) | async-done | bytes 3932176 | tf_op jit(solution)/shard_map/all_gather | solution.py:368
  96.0 30.7 %shard_map.68 = (f32[2048,128]{1,0:T(8,128)}, bf16[2,2048,256]{2,1,0:T(8,128)(2,1)}, bf16[2,2048,256]{2,1,0:T(8,128)(2,1)}) custom-call(s32[16]{0:T(128)} %bitcast.57, s32[1]{0:T(128)} %bitcast.1.place, f32[4,1920,128]{2,1,0:T(8,128)} %bitcast.60), custom_call_target="tpu_custom_call" | custom-call | flops 24999999488 | bytes 9175040 | tf_op jit(solution)/shard_map/pallas_call | solution.py:332
  126.7 28.6 %all-gather.10.cloned.1.call-done = f32[5632,128]{1,0:T(8,128)} async-done(((f32[1408,128]{1,0:T(8,128)}), f32[5632,128]{1,0:T(8,128)}) %all-gather.10.cloned.1.call-update) | async-done | bytes 2883600 | tf_op jit(solution)/shard_map/all_gather | solution.py:368
  155.3 34.2 %shard_map.69 = (f32[2048,128]{1,0:T(8,128)}, bf16[2,1536,256]{2,1,0:T(8,128)(2,1)}, bf16[2,1536,256]{2,1,0:T(8,128)(2,1)}) custom-call(s32[16]{0:T(128)} %bitcast.58, s32[1]{0:T(128)} %bitcast.1.place, f32[4,1408,128]{2,1,0:T(8,128)} %bitcast.61, bf16[2,2048,256]{2,1,0:T(8,128)(2,1)} %get-tuple-element.13.rest_0_, ...), custom_call_target="tpu_custom_call" | custom-call | flops 24999999488 | bytes 11272192 | tf_op jit(solution)/shard_map/pallas_call | solution.py:332
  189.5 0.0 copy-start.4
  189.5 0.0 copy-start.1
  189.5 0.0 copy-start.2
  189.5 10.9 %shard_map.70.rest_4_ = f32[36,128,128]{2,1,0:T(8,128)} custom-call(bf16[2,2048,256]{2,1,0:T(8,128)(2,1)} %get-tuple-element.13.rest_0_, bf16[2,2048,256]{2,1,0:T(8,128)(2,1)} %get-tuple-element.14.rest_1_, bf16[2,1536,256]{2,1,0:T(8,128)(2,1)} %get-tuple-element.16.rest_2_, bf16[2,1536,256]{2,1,0:T(8,128)(2,1)} %get-tuple-element.17.rest_3_), custom_call_target="tpu_custom_call" | custom-call | flops 6000000000 | bytes 9699328 | tf_op jit(solution)/shard_map/pallas_call | solution.py:332
  200.4 0.0 collective-permute-start.3
  200.4 0.0 all-gather.12.cloned.1.call-done
  200.4 0.5 collective-permute-start.1
  200.9 17.9 %all_gather.31.rest_1_ = f32[4,384,128]{2,1,0:T(8,128)S(1)} all-gather(f32[1,384,128]{2,1,0:T(8,128)S(1)} %bitcast.52), channel_id=1, replica_groups=mesh['leaf'=8,'grid'=4] {'grid'}, dimensions={0}, use_global_device_ids=true | all-gather | bytes 983040 | tf_op jit(solution)/shard_map/all_gather | solution.py:368
  218.8 0.0 copy-start.3
  218.8 0.0 collective-permute-start.2
  218.9 0.8 fusion.4
  219.6 0.0 copy-done.4
  219.6 0.1 compare_bitcast_fusion
  219.7 0.1 select_reduce_fusion.1
  219.8 0.7 fusion.2.blocks
  220.5 0.5 broadcast_add_fusion.other_at
  221.0 0.6 broadcast_add_fusion.1.mine_at
  221.6 0.0 copy-done.1
  221.6 0.0 copy-done.2
  221.6 0.1 maximum_bitcast_fusion
  221.7 0.0 copy-done.3
  221.8 10.0 %copy.13 = f32[1,1,2048,2,1,128]{5,4,3,2,1,0:T(1,128)} copy(f32[1,1,2048,2,1,128]{5,2,3,4,1,0:T(8,128)S(1)} %maximum_bitcast_fusion) | data formatting | bytes 4194304
  231.7 0.0 collective-permute-done.2.rest_3_
  231.7 0.0 collective-permute-done.1.rest_2_
  231.7 0.0 collective-permute-done.3.rest_5_
  231.7 67.0 %shard_map.71 = f32[2048,2,1,128]{3,2,1,0:T(1,128)} custom-call(s32[2]{0:T(128)} %fusion.2.blocks, s32[16]{0:T(128)} %broadcast_add_fusion.1.mine_at, s32[16]{0:T(128)} %broadcast_add_fusion.other_at, f32[4,896,128]{2,1,0:T(8,128)} %bitcast.63, f32[4,384,128]{2,1,0:T(8,128)} %copy-done.3, f32[4,896,128]{2,1,0:T(8,128)} %collective-permute-done.1.rest_2_, ...), custom_call_target="tpu_custom_call" | custom-call | flops 49999998976 | bytes 12066816 | tf_op jit(solution)/shard_map/pallas_call | solution.py:332
  (8 shorter events, 0.1 us)
Async XLA Ops:
  7.2 26.6 %copy-start = (s32[4,16]{1,0:T(4,128)S(1)}, s32[4,16]{1,0:T(4,128)}, u32[]{:S(2)}) copy-start(s32[4,16]{1,0:T(4,128)} %param.10) | copy-start | bytes 772
  7.2 88.8 %all-gather.8.cloned.1.call-start = ((), (), s32[]{:S(2)}) async-start(), calls=%async_computation | async-start | bytes 4915200 | tf_op jit(solution)/shard_map/all_gather | solution.py:368
  16.7 3.3 %copy-start.5 = (f32[1,1,2,1,128]{4,3,2,1,0:T(1,128)S(1)}, f32[1,1,2,1,128]{4,3,2,1,0:T(1,128)}, u32[]{:S(2)}) copy-start(f32[1,1,2,1,128]{4,3,2,1,0:T(1,128)} %param.11) | copy-start | bytes 3076
  16.7 138.7 %all-gather.10.cloned.1.call-start = ((), (), s32[]{:S(2)}) async-start(), calls=%async_computation.1 | async-start | bytes 3604480 | tf_op jit(solution)/shard_map/all_gather | solution.py:368
  19.9 180.5 %all-gather.12.cloned.1.call-start = ((), (), s32[]{:S(2)}) async-start(), calls=%async_computation.2 | async-start | bytes 2293760 | tf_op jit(solution)/shard_map/all_gather | solution.py:368
  32.9 2.2 collective-permute-start
  189.5 30.1 %copy-start.4 = (s32[1,1,16]{2,1,0:T(1,128)S(1)}, s32[1,1,16]{2,1,0:T(1,128)}, u32[]{:S(2)}) copy-start(s32[1,1,16]{2,1,0:T(1,128)} %get-tuple-element.37) | copy-start | bytes 196
  189.5 32.1 %copy-start.1 = (f32[2048,128]{1,0:T(8,128)S(1)}, f32[2048,128]{1,0:T(8,128)}, u32[]{:S(2)}) copy-start(f32[2048,128]{1,0:T(8,128)} %get-tuple-element.12) | copy-start | bytes 3145732
  189.5 32.1 %copy-start.2 = (f32[2048,128]{1,0:T(8,128)S(1)}, f32[2048,128]{1,0:T(8,128)}, u32[]{:S(2)}) copy-start(f32[2048,128]{1,0:T(8,128)} %get-tuple-element.15) | copy-start | bytes 3145732
  200.4 31.3 %collective-permute-start.3 = (f32[36,128,128]{2,1,0:T(8,128)}, f32[36,128,128]{2,1,0:T(8,128)}, u32[]{:S(2)}, u32[]{:S(2)}) collective-permute-start(f32[36,128,128]{2,1,0:T(8,128)} %shard_map.70.rest_4_), channel_id=1, source_target_pairs={{0,4},{4,0},{8,12},{12,8},{16,20},{20,16},{24,28},{28,24},{1,5},{5... | collective-permute-start | bytes 7077896 | tf_op jit(solution)/shard_map/ppermute | solution.py:417
  200.4 31.3 %collective-permute-start.1 = (f32[4,896,128]{2,1,0:T(8,128)}, f32[4,896,128]{2,1,0:T(8,128)}, u32[]{:S(2)}, u32[]{:S(2)}) collective-permute-start(f32[4,896,128]{2,1,0:T(8,128)} %bitcast.62), channel_id=1, source_target_pairs={{0,4},{4,0},{8,12},{12,8},{16,20},{20,16},{24,28},{28,24},{1,5},{5... | collective-permute-start | bytes 5505032 | tf_op jit(solution)/shard_map/ppermute | solution.py:418
  218.8 2.9 copy-start.3
  218.8 12.9 %collective-permute-start.2 = (f32[4,384,128]{2,1,0:T(8,128)S(1)}, f32[4,384,128]{2,1,0:T(8,128)}, u32[]{:S(2)}, u32[]{:S(2)}) collective-permute-start(f32[4,384,128]{2,1,0:T(8,128)S(1)} %all_gather.31.rest_1_), channel_id=1, source_target_pairs={{0,4},{4,0},{8,12},{12,8},{16,20},{20,16},{24,28},{28,24},{1,5},{5... | collective-permute-start | bytes 2359304 | tf_op jit(solution)/shard_map/ppermute | solution.py:418
Sparse Core Ops, SparseCore 0:
  16.8 79.1 all-gather.7
  97.6 57.7 all-gather.9
  156.9 40.0 all-gather.11

commit v4 on v3

--- a/solution.py
+++ b/solution.py
@@ -142,15 +142,16 @@
     lax.fori_loop(0, count, step, 0)
 
 
-def entry_block(entries, grid_count, row, col):
+def entry_block(entries, grid_count, row, col, first=0):
     most = grid_count // 2
     if row >= grid_count:
-        at = most + 1 + row - grid_count
+        at = first + most + 1 + row - grid_count
         return entries[col, at * NB : (at + 1) * NB, :]
     at = row - col
     if at <= most:
+        at += first
         return entries[col, at * NB : (at + 1) * NB, :]
-    at = grid_count - at
+    at = first + grid_count - at
     return entries[row, at * NB : (at + 1) * NB, :].T
 
 
@@ -243,16 +244,23 @@
         lax.fori_loop(q, CB // 2, tile, 0)
 
 
-def parent_kernel(slots, grid_count, late, blocks, mine_at, other_at, *rest):
-    my_entries, other_entries = rest[:late], rest[late : 2 * late]
-    my_product, other_product, diagonal, out = rest[2 * late : 2 * late + 4]
-    mine, other, own, front, high, low, block, inverse, sems = rest[2 * late + 4 :]
+def parent_kernel(slots, grid_count, firsts, blocks, mine_at, other_at, *rest):
+    my_entries, other_entries, my_product, other_product, diagonal = rest[:5]
+    owned = rest[5 : len(rest) - 11]
+    out, child_out, mine, other, own, front, high, low, block, inverse, sems = rest[len(rest) - 11 :]
+    child_copies = [
+        pltpu.make_async_copy(part, child_out.at[:, t, 0, :], sems.at[slots + t]) for t, part in enumerate(owned)
+    ]
+    for copy in child_copies:
+        copy.start()
     for schur, entries, product in ((mine, my_entries, my_product), (other, other_entries, other_product)):
         for c in range(CB):
             t, inner = divmod(c, grid_count)
             for r in range(c, CB):
                 at = packed_at(r, c)
-                schur[at] = entry_block(entries[t], grid_count, r - t * grid_count, inner) - product[at]
+                schur[at] = entry_block(
+                    entries, grid_count, r - t * grid_count, inner, firsts[t]
+                ) - product[at]
     row_id = lax.broadcasted_iota(jnp.int32, (NB, NB), 0)
     col_id = lax.broadcasted_iota(jnp.int32, (NB, NB), 1)
     own[...] = jnp.zeros_like(own)
@@ -323,21 +331,21 @@
     copies = [pltpu.make_async_copy(own.at[s], out.at[:, s, 0, :], sems.at[s]) for s in range(slots)]
     for copy in copies:
         copy.start()
-    for copy in copies:
+    for copy in copies + child_copies:
         copy.wait()
 
 
-def call(kernel, outs, scratch, smem, vmem, flops, out_space=pltpu.VMEM):
+def call(kernel, outs, scratch, smem, vmem, flops, out_space=pltpu.VMEM, passed=()):
     size = sum(a.size * a.dtype.itemsize for a in vmem) + sum(a.size * a.dtype.itemsize for a in outs)
     return pl.pallas_call(
         kernel,
         out_shape=outs,
-        in_specs=[SMEM] * len(smem) + [VMEM] * len(vmem),
+        in_specs=[SMEM] * len(smem) + [VMEM] * len(vmem) + [pl.BlockSpec(memory_space=pl.ANY)] * len(passed),
         out_specs=[pl.BlockSpec(memory_space=out_space)] * len(outs),
         scratch_shapes=scratch,
         compiler_params=pltpu.CompilerParams(vmem_limit_bytes=LIMIT),
         cost_estimate=pl.CostEstimate(flops=flops, bytes_accessed=size, transcendentals=0),
-    )(*smem, *vmem)
+    )(*smem, *vmem, *passed)
 
 
 def shape(dims, dtype=f32):
@@ -365,7 +373,10 @@
         near = jnp.take(near, half_ring, axis=0).reshape(-1, NB)
         return jnp.concatenate([near, entries[base + grid_count * NB :, t, :]], axis=0)
 
-    gathered = [lax.all_gather(sent(t), "grid", axis=0) for t in range(rounds)]
+    gathered = [lax.all_gather(sent(t), "grid", axis=0) for t in range(pivot_rounds)]
+    late_sent = [sent(t) for t in range(pivot_rounds, rounds)]
+    firsts = [sum(part.shape[0] for part in late_sent[:t]) // NB for t in range(len(late_sent))]
+    late = lax.all_gather(jnp.concatenate(late_sent, axis=0), "grid", axis=0)
 
     my_live = lax.dynamic_index_in_dim(child_live, leaf_pos, 0, keepdims=False)[0]
     other_live = lax.dynamic_index_in_dim(child_live, sibling, 0, keepdims=False)[0]
@@ -404,7 +415,6 @@
         )
         owned.append(own)
         done += [high, low]
-    late = gathered[pivot_rounds:]
     lower = CB * (CB + 1) // 2
     (mine,) = call(
         functools.partial(product_kernel, pivot_rounds, grid_count),
@@ -415,11 +425,11 @@
         6_000_000_000,
     )
     other = lax.ppermute(mine, "leaf", swap)
-    other_late = [lax.ppermute(part, "leaf", swap) for part in late]
+    other_late = lax.ppermute(late, "leaf", swap)
     packed = (PB // 2, F, PAIR)
-    (parent,) = call(
-        functools.partial(parent_kernel, slots, grid_count, len(late)),
-        [shape((F, slots, 1, NB))],
+    parent, child_factor = call(
+        functools.partial(parent_kernel, slots, grid_count, firsts),
+        [shape((F, slots, 1, NB)), shape((F, pivot_rounds, 1, NB))],
         [
             pltpu.VMEM((lower, NB, NB), f32),
             pltpu.VMEM((lower, NB, NB), f32),
@@ -429,14 +439,14 @@
             pltpu.VMEM(packed, bf16),
             pltpu.VMEM((NB, NB), f32),
             pltpu.VMEM((NB, NB), f32),
-            pltpu.SemaphoreType.DMA((slots,)),
+            pltpu.SemaphoreType.DMA((slots + pivot_rounds,)),
         ],
         [parent_blocks, sources(my_map, my_live), sources(other_map, other_live)],
-        [*late, *other_late, mine, other, diagonal],
+        [late, other_late, mine, other, diagonal],
         50_000_000_000,
         pl.ANY,
+        owned,
     )
-    child_factor = jnp.stack(owned, axis=1)
     return (
         child_factor.reshape(1, 1, F, pivot_rounds, 1, NB),
         parent.reshape(1, 1, F, slots, 1, NB),

time: 308 us -> 334 us (1.084)
  waiting for transfers between devices: 88.9 us -> 145 us
  blocking collectives: 30.8 us -> 12.9 us
  local copies, waits for them, and re-layouts: 22.3 us -> 12.3 us
    all_gather x3, waiting for transfers between devices: 88.8 us -> 142 us  [the longest x2 106 us: body(): lax.all_gather(sent(t), 'grid', axis=0)]
    all_gather x1 -> x0, blocking collectives: 17.9 us -> none  [body(): gathered = [lax.all_gather(sent(t), 'grid', axis=0) for t in range(rounds)]]
    unnamed x13 -> x8, local copies, waits for them, and re-layouts: 10 us -> 0.02 us
  transfers between devices with their start and end apart: 7 -> 6, of which waited for: 2 -> 4; matrix products, arithmetic and copies ran while one was open for 6% -> 3% of each run, Pallas kernels for 25% -> 23%
where the time goes in v4:
time: 334 us
  waiting for transfers between devices  145 us (43%)
  Pallas kernels  144 us (43%)
  between operations  13.9 us (4%)
  blocking collectives  12.9 us (4%)
  local copies, waits for them, and re-layouts  12.3 us (4%)
  other arithmetic  5.72 us (2%)
    pallas_call x4, Pallas kernels, call(): pl.pallas_call(kernel, out_shape=outs, in_specs=[SMEM] * len(smem) + [VME...  144 us
    all_gather x2, waiting for transfers between devices, body(): lax.all_gather(sent(t), 'grid', axis=0)  106 us
    all_gather x1, waiting for transfers between devices, body(): late = lax.all_gather(jnp.concatenate(late_sent, axis=0), 'grid', axis=0)  36.3 us
    all_gather x1, blocking collectives, body(): shifts = lax.all_gather(parent_shift.reshape(slots, NB), 'grid', axis=0)  12.9 us
  transfers between devices with their start and end apart: 6, of which 4 were waited for; matrix products, arithmetic and copies ran while one was open for 3% of the time, Pallas kernels for 23%

profile of v4, /device:TPU:0, one launch (start us, length us, event | category | flops | bytes accessed | tf_op | source)
XLA Modules:
  0.0 334.0 jit_solution(3428890423680884139)
XLA Ops:
  7.2 0.0 copy-start
  7.2 0.0 all-gather.8.cloned.1.call-start
  7.3 3.8 %fusion.7 = (f32[512,1,128]{2,1,0:T(1,128)S(1)}, f32[512,1,128]{2,1,0:T(1,128)S(1)}, f32[512,1,128]{2,1,0:T(1,128)S(1)}, f32[512,1,128]{2,1,0:T(1,128)S(1)}, f32[512,1,128]{2,1,0:T(1,128)S(1)}) fusion(f32[2048,4,128]{2,1,0:T(4,128)} %bitcast.40), kind=kLoop, calls=%fused_computation.45 | loop fusion | bytes 2621440 | tf_op jit(solution)/shard_map/slice | solution.py:372
  11.1 0.6 gather_fusion.3
  11.7 0.6 gather_fusion.2
  12.3 0.6 gather_fusion.1
  12.8 0.6 gather_fusion
  13.4 0.1 broadcast_select_fusion
  13.5 0.9 pad_maximum_fusion.2
  14.4 0.0 all-gather.8.cloned.1.call-update
  14.5 0.0 all-gather.10.cloned.1.call-start
  14.5 2.2 slice.50
  16.7 1.0 pad_maximum_fusion
  17.7 0.0 copy-start.2
  17.7 0.0 all-gather.10.cloned.1.call-update
  17.7 0.0 all-gather.12.cloned.1.call-start
  17.8 2.1 slice.52
  19.9 0.9 pad_maximum_fusion.1
  20.8 0.0 all-gather.12.cloned.1.call-update
  20.8 0.0 copy-done.2
  20.8 12.9 %all-gather.2 = f32[4,1,2,1,128]{4,2,3,1,0:T(2,128)S(1)} all-gather(f32[1,1,2,1,128]{4,2,3,1,0:T(2,128)S(1)} %bitcast.56), channel_id=4, replica_groups=mesh['leaf'=8,'grid'=4] {'grid'}, dimensions={0}, use_global_device_ids=true | all-gather | bytes 5120 | tf_op jit(solution)/shard_map/all_gather | solution.py:367
  33.8 0.0 collective-permute-start.1
  33.8 0.0 copy-done
  33.8 0.1 iota_compare_fusion
  33.9 1.2 constant_dynamic-slice_fusion.2
  35.1 0.0 collective-permute-done.1
  35.1 0.7 select_reduce_fusion.rest_4_
  35.9 36.3 %all-gather.8.cloned.1.call-done = f32[5120,128]{1,0:T(8,128)} async-done(((f32[1280,128]{1,0:T(8,128)}), f32[5120,128]{1,0:T(8,128)}) %all-gather.8.cloned.1.call-update) | async-done | bytes 2621456 | tf_op jit(solution)/shard_map/all_gather | solution.py:379
  72.1 0.0 collective-permute-start
  72.1 77.4 %all-gather.10.cloned.1.call-done = f32[7680,128]{1,0:T(8,128)} async-done(((f32[1920,128]{1,0:T(8,128)}), f32[7680,128]{1,0:T(8,128)}) %all-gather.10.cloned.1.call-update) | async-done | bytes 3932176 | tf_op jit(solution)/shard_map/all_gather | solution.py:376
  149.5 30.7 %shard_map.68 = (f32[2048,128]{1,0:T(8,128)}, bf16[2,2048,256]{2,1,0:T(8,128)(2,1)}, bf16[2,2048,256]{2,1,0:T(8,128)(2,1)}) custom-call(s32[16]{0:T(128)} %bitcast.54, s32[1]{0:T(128)} %bitcast.13.place, f32[4,1920,128]{2,1,0:T(8,128)} %bitcast.57), custom_call_target="tpu_custom_call" | custom-call | flops 24999999488 | bytes 9175040 | tf_op jit(solution)/shard_map/pallas_call | solution.py:340
  180.2 28.7 %all-gather.12.cloned.1.call-done = f32[5632,128]{1,0:T(8,128)} async-done(((f32[1408,128]{1,0:T(8,128)}), f32[5632,128]{1,0:T(8,128)}) %all-gather.12.cloned.1.call-update) | async-done | bytes 2883600 | tf_op jit(solution)/shard_map/all_gather | solution.py:376
  208.9 34.3 %shard_map.69 = (f32[2048,128]{1,0:T(8,128)}, bf16[2,1536,256]{2,1,0:T(8,128)(2,1)}, bf16[2,1536,256]{2,1,0:T(8,128)(2,1)}) custom-call(s32[16]{0:T(128)} %bitcast.55, s32[1]{0:T(128)} %bitcast.13.place, f32[4,1408,128]{2,1,0:T(8,128)} %bitcast.58, bf16[2,2048,256]{2,1,0:T(8,128)(2,1)} %get-tuple-element.14.rest_0_, ...), custom_call_target="tpu_custom_call" | custom-call | flops 24999999488 | bytes 11272192 | tf_op jit(solution)/shard_map/pallas_call | solution.py:340
  243.2 0.0 copy-start.1
  243.2 10.8 %shard_map.70.rest_2_ = f32[36,128,128]{2,1,0:T(8,128)} custom-call(bf16[2,2048,256]{2,1,0:T(8,128)(2,1)} %get-tuple-element.14.rest_0_, bf16[2,2048,256]{2,1,0:T(8,128)(2,1)} %get-tuple-element.15.rest_1_, bf16[2,1536,256]{2,1,0:T(8,128)(2,1)} %get-tuple-element.16.rest_2_, bf16[2,1536,256]{2,1,0:T(8,128)(2,1)} %get-tuple-element.17.rest_3_), custom_call_target="tpu_custom_call" | custom-call | flops 6000000000 | bytes 9699328 | tf_op jit(solution)/shard_map/pallas_call | solution.py:340
  254.0 0.0 collective-permute-start.2
  254.0 0.7 fusion.4
  254.6 0.7 fusion.2.blocks
  255.4 0.0 copy-done.1
  255.4 0.1 compare_bitcast_fusion
  255.4 0.1 select_reduce_fusion.1
  255.5 0.5 broadcast_add_fusion.other_at
  256.0 0.6 broadcast_add_fusion.1.mine_at
  256.6 0.0 collective-permute-done.rest_1_
  256.6 0.0 copy-start.3
  256.6 2.2 collective-permute-done.2.rest_3_
  258.8 0.0 copy-done.3
  258.8 68.6 %shard_map.71 = (f32[2048,2,1,128]{3,2,1,0:T(1,128)}, f32[2048,2,1,128]{3,2,1,0:T(1,128)}) custom-call(s32[2]{0:T(128)} %fusion.2.blocks, s32[16]{0:T(128)} %broadcast_add_fusion.1.mine_at, s32[16]{0:T(128)} %broadcast_add_fusion.other_at, f32[4,1280,128]{2,1,0:T(8,128)} %bitcast.60, f32[4,1280,128]{2,1,0:T(8,128)} %copy-done.3, ...), custom_call_target="tpu_custom_call" | custom-call | flops 49999998976 | bytes 14163968 | tf_op jit(solution)/shard_map/pallas_call | solution.py:340
  (8 shorter events, 0.1 us)
Async XLA Ops:
  7.2 26.6 %copy-start = (s32[4,16]{1,0:T(4,128)S(1)}, s32[4,16]{1,0:T(4,128)}, u32[]{:S(2)}) copy-start(s32[4,16]{1,0:T(4,128)} %param.10) | copy-start | bytes 772
  7.2 64.9 %all-gather.8.cloned.1.call-start = ((), (), s32[]{:S(2)}) async-start(), calls=%async_computation | async-start | bytes 3276800 | tf_op jit(solution)/shard_map/all_gather | solution.py:379
  14.5 135.1 %all-gather.10.cloned.1.call-start = ((), (), s32[]{:S(2)}) async-start(), calls=%async_computation.1 | async-start | bytes 4915200 | tf_op jit(solution)/shard_map/all_gather | solution.py:376
  17.7 3.1 copy-start.2
  17.7 191.2 %all-gather.12.cloned.1.call-start = ((), (), s32[]{:S(2)}) async-start(), calls=%async_computation.2 | async-start | bytes 3604480 | tf_op jit(solution)/shard_map/all_gather | solution.py:376
  33.8 1.3 collective-permute-start.1
  72.1 184.5 %collective-permute-start = (f32[4,1280,128]{2,1,0:T(8,128)}, f32[4,1280,128]{2,1,0:T(8,128)S(1)}, u32[]{:S(2)}, u32[]{:S(2)}) collective-permute-start(f32[4,1280,128]{2,1,0:T(8,128)} %bitcast.59), channel_id=1, source_target_pairs={{0,4},{4,0},{8,12},{12,8},{16,20},{20,16},{24,28},{28,24},{1,5},{5... | collective-permute-start | bytes 7864328 | tf_op jit(solution)/shard_map/ppermute | solution.py:428
  243.2 12.2 %copy-start.1 = (s32[1,1,16]{2,1,0:T(1,128)S(1)}, s32[1,1,16]{2,1,0:T(1,128)}, u32[]{:S(2)}) copy-start(s32[1,1,16]{2,1,0:T(1,128)} %get-tuple-element.40) | copy-start | bytes 196
  254.0 4.9 %collective-permute-start.2 = (f32[36,128,128]{2,1,0:T(8,128)}, f32[36,128,128]{2,1,0:T(8,128)}, u32[]{:S(2)}, u32[]{:S(2)}) collective-permute-start(f32[36,128,128]{2,1,0:T(8,128)} %shard_map.70.rest_2_), channel_id=1, source_target_pairs={{0,4},{4,0},{8,12},{12,8},{16,20},{20,16},{24,28},{28,24},{1,5},{5... | collective-permute-start | bytes 7077896 | tf_op jit(solution)/shard_map/ppermute | solution.py:427
  256.6 2.2 copy-start.3
Sparse Core Ops, SparseCore 0:
  14.6 57.4 all-gather.7
  74.3 75.2 all-gather.9
  151.1 57.7 all-gather.11
